TPU v7x, 128 devices: a whole 4x4x4 slice. The times are simulated.
128 devices in a mesh: enc: 4 (over x), seq: 32 (over y, z, core).
Axes of the slice: x: 4, y: 4, z: 4, core: 2. Of those that a mesh axis runs over, the one named last changes fastest.
Arguments:
- queries: bfloat16 [28672, 4096], P('seq', 'enc'), may hold values from -180 to 180
- d_attended: bfloat16 [28672, 4096], P('seq', 'enc'), may hold values from -5 to 5
- encodings: bfloat16 [64, 128, 4096], P('seq'), may hold values from -6 to 6
- w_key: bfloat16 [4096, 4096], P(None, 'enc'), may hold values from -0.09375 to 0.09375
- w_value: bfloat16 [4096, 4096], P(None, 'enc'), may hold values from -0.09375 to 0.09375
- neighbour_owner: int32 [448, 2], P('seq'), may hold values from 0 to 31, all different within a row; in each aligned block of 14 rows (0 to 13, 14 to 27, ...) at most 2 rows name the same one
- neighbour_slot: int32 [448, 2], P('seq'), may hold values from 0 to 1
Outputs:
- attended: bfloat16 [28672, 4096], P('seq', 'enc')
- d_queries: bfloat16 [28672, 4096], P('seq', 'enc')
- d_encodings: bfloat16 [64, 128, 4096], P('seq', None, 'enc')
Inputs may be any that keep to these rules, and one draw needn't show every extreme that they name: `neighbour_owner`: the two owners of a span differ. Among the 14 spans of one device (aligned blocks of rows), no owner is named more than 2 times, and in some block one owner is named exactly 2 times.
All inputs are finite; a program needn't handle non-finite values.
Results may differ from a plain program's by a relative error of at most 0.013.
The roundings to bfloat16 on the way count: a program that leaves them out, or rounds other values in their place, can miss the bound.
Values may be sent and summed in bfloat16 or wider, within the bound.
A program may use at most 256 MiB of HBM per device.

v0:
```python
import math

import jax
import jax.numpy as jnp
from jax import lax
from jax.sharding import PartitionSpec as P

HD = 128
SPAN = 64
NBR_LEN = 128


def shifted(value, axis, steps):
    count = lax.axis_size(axis)
    first, last = (max(0, -steps), min(count, count - steps))
    return lax.ppermute(value, axis, [(source, source + steps) for source in range(first, last)])


def split_heads(row_block, head_count):
    return row_block.reshape(row_block.shape[:-1] + (head_count, row_block.shape[-1] // head_count))


def slot_scores(asked_rows, key_block, head_count):
    query_heads = split_heads(asked_rows, head_count)
    key_heads = split_heads(key_block, head_count)
    return jnp.einsum(
        "abthd,abrhd->abhtr", query_heads, key_heads, preferred_element_type=jnp.float32
    ) * (1.0 / math.sqrt(HD))


def per_device(queries, d_attended, encodings, w_key, w_value, neighbour_owner, neighbour_slot):
    seq_count = lax.axis_size("seq")
    tok_rows, feat_width = queries.shape
    head_count = feat_width // HD
    span_count = tok_rows // SPAN
    read_count = 2 * span_count
    capacity = max(2, (2 * span_count + seq_count - 1) // seq_count)
    slot_count = seq_count * capacity
    margin = SPAN - 1
    owned_count = encodings.shape[0]
    score_scale = 1.0 / math.sqrt(HD)
    rim_rows = shifted(jnp.stack([queries[:margin], d_attended[:margin]]), "seq", -1)
    query_shift = jnp.concatenate([queries[margin:], rim_rows[0]], axis=0)
    grad_shift = jnp.concatenate([d_attended[margin:], rim_rows[1]], axis=0)
    enc_flat = encodings.reshape(owned_count * NBR_LEN, encodings.shape[2])
    key_table = (
        jnp.dot(enc_flat, w_key, preferred_element_type=jnp.float32)
        .astype(jnp.bfloat16)
        .reshape(owned_count, NBR_LEN, feat_width)
    )
    value_table = (
        jnp.dot(enc_flat, w_value, preferred_element_type=jnp.float32)
        .astype(jnp.bfloat16)
        .reshape(owned_count, NBR_LEN, feat_width)
    )
    owners = neighbour_owner.reshape(read_count)
    slot_picks = neighbour_slot.reshape(read_count)
    owner_hot = (owners[:, None] == jnp.arange(seq_count, dtype=jnp.int32)[None, :]).astype(
        jnp.int32
    )
    earlier = jnp.cumsum(owner_hot, axis=0) - owner_hot
    slot_rank = jnp.sum(earlier * owner_hot, axis=1)
    slot_place = owners * capacity + slot_rank
    slot_match = jnp.arange(slot_count, dtype=jnp.int32)[:, None] == slot_place[None, :]
    span_match = jnp.sum(slot_match.reshape(slot_count, span_count, 2).astype(jnp.float32), axis=2)
    wanted_ids = (
        jnp.sum(jnp.where(slot_match, slot_picks[None, :], 0), axis=1)
        .astype(jnp.bfloat16)
        .reshape(seq_count, capacity)
    )

    def to_slots(span_rows):
        spread = jnp.dot(
            span_match.astype(jnp.bfloat16),
            span_rows.reshape(span_count, SPAN * feat_width),
            preferred_element_type=jnp.float32,
        )
        return spread.astype(jnp.bfloat16).reshape(seq_count, capacity, SPAN, feat_width)

    def stats_to_slots(stat_rows):
        spread = jnp.dot(
            span_match,
            stat_rows.reshape(span_count, head_count * SPAN),
            precision=lax.Precision.HIGHEST,
        )
        return spread.reshape(seq_count, capacity, head_count, SPAN)

    query_slots = to_slots(query_shift)
    received = (
        lax.all_to_all(query_slots, "seq", split_axis=0, concat_axis=0, tiled=True),
        lax.all_to_all(wanted_ids, "seq", split_axis=0, concat_axis=0, tiled=True),
    )
    asked_rows = received[0]
    wanted = received[1].astype(jnp.int32)
    slot_score = slot_scores(asked_rows, key_table[wanted], head_count)
    part_lse = jax.nn.logsumexp(slot_score, axis=-1)
    prob_round = jnp.exp(slot_score - part_lse[..., None]).astype(jnp.bfloat16)
    part_out = jnp.einsum(
        "abhtr,abrhd->abthd",
        prob_round,
        split_heads(value_table[wanted], head_count),
        preferred_element_type=jnp.float32,
    )
    part_out = part_out.astype(jnp.bfloat16).reshape(asked_rows.shape)
    part_back = lax.all_to_all(
        part_out.astype(jnp.float32), "seq", split_axis=0, concat_axis=0, tiled=True
    ).astype(part_out.dtype)
    lse_back = lax.all_to_all(part_lse, "seq", split_axis=0, concat_axis=0, tiled=True)
    part_back, lse_back, asked_rows, wanted_kept = (
        part_back,
        lse_back,
        asked_rows,
        received[1],
    ) + tuple(received[2:])
    part_rows = jnp.take(
        part_back.reshape(slot_count, SPAN * feat_width), slot_place, axis=0
    ).reshape(span_count, 2, SPAN, head_count, HD)
    lse_rows = jnp.take(
        lse_back.reshape(slot_count, head_count * SPAN), slot_place, axis=0
    ).reshape(span_count, 2, head_count, SPAN)
    lse_total = jnp.logaddexp(lse_rows[:, 0], lse_rows[:, 1])
    share_rows = jnp.exp(lse_rows - lse_total[:, None]).transpose(0, 1, 3, 2)[..., None]
    merged = share_rows[:, 0] * part_rows[:, 0].astype(jnp.float32) + share_rows[:, 1] * part_rows[
        :, 1
    ].astype(jnp.float32)
    attended_shift = merged.astype(jnp.bfloat16).reshape(tok_rows, feat_width)
    attended_tail = shifted(attended_shift[tok_rows - margin :], "seq", 1)
    delta_rows = jnp.sum(
        grad_shift.reshape(span_count, SPAN, head_count, HD).astype(jnp.float32) * merged, axis=-1
    ).transpose(0, 2, 1)
    total_slots = stats_to_slots(lse_total)
    delta_slots = stats_to_slots(delta_rows)
    grad_slots = to_slots(grad_shift)
    grads_in, total_got, delta_got = (
        lax.all_to_all(
            grad_slots.astype(jnp.float32), "seq", split_axis=0, concat_axis=0, tiled=True
        ).astype(grad_slots.dtype),
        lax.all_to_all(total_slots, "seq", split_axis=0, concat_axis=0, tiled=True),
        lax.all_to_all(delta_slots, "seq", split_axis=0, concat_axis=0, tiled=True),
    )
    wanted = wanted_kept.astype(jnp.int32)
    key_block = key_table[wanted]
    value_heads = split_heads(value_table[wanted], head_count)
    key_heads = split_heads(key_block, head_count)
    asked_heads = split_heads(asked_rows, head_count)
    grad_heads = split_heads(grads_in, head_count)
    slot_score = slot_scores(asked_rows, key_block, head_count)
    full_prob = jnp.exp(slot_score - total_got[..., None])
    full_round = full_prob.astype(jnp.bfloat16)
    prob_grad = jnp.einsum(
        "abthd,abrhd->abhtr", grad_heads, value_heads, preferred_element_type=jnp.float32
    )
    score_grad = (full_prob * (prob_grad - delta_got[..., None]) * score_scale).astype(jnp.bfloat16)
    query_part = jnp.einsum(
        "abhtr,abrhd->abthd", score_grad, key_heads, preferred_element_type=jnp.float32
    )
    query_part = query_part.astype(jnp.bfloat16).reshape(asked_rows.shape)
    grad_back = lax.all_to_all(query_part, "seq", split_axis=0, concat_axis=0, tiled=True)
    store_hot = (wanted[..., None] == jnp.arange(owned_count, dtype=jnp.int32)).astype(jnp.bfloat16)
    asked_sel = asked_heads[:, :, None] * store_hot[:, :, :, None, None, None]
    grads_sel = grad_heads[:, :, None] * store_hot[:, :, :, None, None, None]
    key_grad = jnp.einsum(
        "abhtr,abnthd->nrhd", score_grad, asked_sel, preferred_element_type=jnp.float32
    )
    key_grad = key_grad.astype(jnp.bfloat16).reshape(owned_count * NBR_LEN, feat_width)
    value_grad = jnp.einsum(
        "abhtr,abnthd->nrhd", full_round, grads_sel, preferred_element_type=jnp.float32
    )
    value_grad = value_grad.astype(jnp.bfloat16).reshape(owned_count * NBR_LEN, feat_width)
    contract = (((1,), (1,)), ((), ()))
    first = lax.dot_general(w_key, key_grad, contract, preferred_element_type=jnp.float32)
    enc_share = lax.psum_scatter(
        first + lax.dot_general(w_value, value_grad, contract, preferred_element_type=jnp.float32),
        "enc",
        scatter_dimension=0,
        tiled=True,
    )
    d_encodings = enc_share.T.astype(jnp.bfloat16).reshape(owned_count, NBR_LEN, enc_share.shape[0])
    grad_rows = jnp.take(
        grad_back.reshape(slot_count, SPAN * feat_width), slot_place, axis=0
    ).reshape(span_count, 2, SPAN * feat_width)
    query_shift_grad = (
        (grad_rows[:, 0].astype(jnp.float32) + grad_rows[:, 1].astype(jnp.float32))
        .astype(jnp.bfloat16)
        .reshape(tok_rows, feat_width)
    )
    query_tail = shifted(query_shift_grad[tok_rows - margin :], "seq", 1)
    attended = jnp.concatenate([attended_tail, attended_shift[: tok_rows - margin]], axis=0)
    d_queries = jnp.concatenate([query_tail, query_shift_grad[: tok_rows - margin]], axis=0)
    return (attended, d_queries, d_encodings)


def solution(mesh):
    return jax.shard_map(
        per_device,
        mesh=mesh,
        in_specs=(
            P("seq", "enc"),
            P("seq", "enc"),
            P("seq", None, None),
            P(None, "enc"),
            P(None, "enc"),
            P("seq", None),
            P("seq", None),
        ),
        out_specs=(P("seq", "enc"), P("seq", "enc"), P("seq", None, "enc")),
        check_vma=False,
    )
```

profile of v0, /device:TPU:1, one launch (start us, length us, event | category | flops | bytes accessed | tf_op | source)
XLA Modules:
  0.0 825.5 jit_solution(9505304944907353011)
XLA Ops:
  10.2 9.6 %all-to-all-start.1 = ((bf16[32,1,2]{2,1,0:T(2,128)(2,1)}), bf16[32,1,2]{2,1,0:T(2,128)(2,1)S(1)}, u32[]{:S(2)}, u32[]{:S(2)}) async-start(bf16[32,1,2]{2,1,0:T(2,128)(2,1)} %convert_element_type.232), calls=%async_computation.1 | async-start | bytes 32768 | tf_op jit(solution)/shard_map/all_to_all | solution.py:91
  41.8 11.6 %copy.235 = bf16[8,8,64,1024]{3,2,1,0:T(8,128)(2,1)} copy(bf16[8,8,64,1024]{3,1,2,0:T(8,128)(2,1)} %bitcast.243) | data formatting | bytes 16777216
  53.5 9.7 %all-to-all-start = ((bf16[32,2,64,1024]{3,2,1,0:T(8,128)(2,1)}), bf16[32,2,64,1024]{3,2,1,0:T(8,128)(2,1)}, u32[]{:S(2)}, u32[]{:S(2)}) async-start(bf16[32,2,64,1024]{3,2,1,0:T(8,128)(2,1)} %bitcast.240), calls=%async_computation | async-start | bytes 16777216 | tf_op jit(solution)/shard_map/all_to_all | solution.py:90
  82.3 21.9 %copy.180 = bf16[64,128,1024]{1,2,0:T(8,128)(2,1)} copy(bf16[64,128,1024]{2,1,0:T(8,128)(2,1)} %gather_fusion.2) | data formatting | bytes 33554432 | tf_op jit(solution)/shard_map/gather | solution.py:101
  111.5 21.8 %copy.175 = bf16[64,128,1024]{1,2,0:T(8,128)(2,1)} copy(bf16[64,128,1024]{2,1,0:T(8,128)(2,1)} %gather_fusion) | data formatting | bytes 33554432 | tf_op jit(solution)/shard_map/gather | solution.py:95
  133.3 38.5 %all-to-all-done = bf16[32,2,64,1024]{3,2,1,0:T(8,128)(2,1)} async-done(((bf16[32,2,64,1024]{3,2,1,0:T(8,128)(2,1)}), bf16[32,2,64,1024]{3,2,1,0:T(8,128)(2,1)}, u32[]{:S(2)}, u32[]{:S(2)}) %all-to-all-start) | async-done | bytes 8388640 | tf_op jit(solution)/shard_map/all_to_all | solution.py:90
  171.8 14.4 %multiply_reduce_fusion = (f32[32,2,8,64]{3,2,1,0:T(8,128)S(1)}, f32[32,2,8,64,128]{4,3,2,1,0:T(8,128)}) fusion(bf16[32,2,128,8,128]{2,4,3,1,0:T(8,128)(2,1)} %bitcast.232, bf16[32,2,64,1024]{3,2,1,0:T(8,128)(2,1)} %all-to-all-done), kind=kOutput, calls=%fused_computation.19 | convolution fusion | flops 1082097664 | bytes 42074112 | tf_op jit(solution)/shard_map/abthd,abrhd->abhtr/dot_general | solution.py:26
  186.1 11.1 %exponential_reduce_fusion = f32[32,2,8,64]{3,2,1,0:T(8,128)S(1)} fusion(f32[32,2,8,64,128]{4,3,2,1,0:T(8,128)} %get-tuple-element.19, f32[32,2,8,64]{3,2,1,0:T(8,128)S(1)} %is-finite_select_fusion), kind=kLoop, calls=%fused_computation.17 | loop fusion | flops 12550144 | bytes 17039360 | tf_op jit(solution)/shard_map/reduce_sum | solution.py:96
  198.1 20.9 %all-to-all-start.2 = ((f32[32,1,1024]{2,1,0:T(1,128)}), f32[32,1,1024]{2,1,0:T(1,128)S(1)}, u32[]{:S(2)}, u32[]{:S(2)}) async-start(f32[32,1,1024]{2,1,0:T(1,128)} %reshape.338), calls=%async_computation.2 | async-start | bytes 262144 | tf_op jit(solution)/shard_map/all_to_all | solution.py:108
  219.0 19.1 %convert_bitcast_fusion = bf16[32,2,8,8,8,128]{5,4,3,2,1,0:T(8,128)(2,1)} fusion(bf16[32,2,128,8,128]{2,4,3,1,0:T(8,128)(2,1)} %bitcast.236, f32[32,2,8,64,128]{4,3,2,1,0:T(8,128)} %get-tuple-element.19, f32[32,2,8,64]{3,2,1,0:T(8,128)S(1)} %log_add_fusion), kind=kOutput, calls=%fused_computation.9 | convolution fusion | flops 1090519040 | bytes 42074112 | tf_op jit(solution)/shard_map/abhtr,abrhd->abthd/dot_general | solution.py:98
  238.0 9.0 %copy.299 = bf16[32,2,8,8,8,128]{5,4,2,3,1,0:T(8,128)(2,1)} copy(bf16[32,2,8,8,8,128]{5,4,3,2,1,0:T(8,128)(2,1)} %convert_bitcast_fusion) | data formatting | bytes 16777216 | tf_op jit(solution)/shard_map/convert_element_type | solution.py:106
  268.4 94.7 %all-to-all-done.3 = bf16[32,2,64,1024]{3,2,1,0:T(8,128)(2,1)} async-done(((bf16[32,2,64,1024]{3,2,1,0:T(8,128)(2,1)}), bf16[32,2,64,1024]{3,2,1,0:T(8,128)(2,1)}, u32[]{:S(2)}, u32[]{:S(2)}) %all-to-all-start.3) | async-done | bytes 8388640 | tf_op jit(solution)/shard_map/all_to_all | solution.py:105
  363.1 21.7 %all-to-all-start.4 = ((f32[32,1,1024]{2,1,0:T(1,128)}), f32[32,1,1024]{2,1,0:T(1,128)}, u32[]{:S(2)}, u32[]{:S(2)}) async-start(f32[32,1,1024]{2,1,0:T(1,128)} %reshape.342), calls=%async_computation.4 | async-start | bytes 262144 | tf_op jit(solution)/shard_map/all_to_all | solution.py:138
  384.8 11.9 %copy.237 = bf16[8,8,64,1024]{3,1,2,0:T(8,128)(2,1)} copy(bf16[8,8,64,1024]{3,2,1,0:T(8,128)(2,1)} %bitcast.69) | data formatting | bytes 16777216
  396.7 12.8 %gather_fusion.3 = bf16[28,65536]{1,0:T(8,128)(2,1)} fusion(bf16[64,65536]{1,0:T(8,128)(2,1)} %bitcast.235, s32[1024]{0:T(1024)S(1)} %pad_clamp_fusion), kind=kCustom, calls=%fused_computation.clone | custom fusion | bytes 7340144 | tf_op jit(solution)/shard_map/jit(_take)/gather | solution.py:115
  433.6 11.6 %copy.242 = bf16[8,8,64,1024]{3,2,1,0:T(8,128)(2,1)} copy(bf16[8,8,64,1024]{3,1,2,0:T(8,128)(2,1)} %bitcast.242) | data formatting | bytes 16777216
  445.2 7.9 all-to-all-start.5
  456.1 105.6 %all-to-all-done.5 = bf16[32,2,64,1024]{3,2,1,0:T(8,128)(2,1)} async-done(((bf16[32,2,64,1024]{3,2,1,0:T(8,128)(2,1)}), bf16[32,2,64,1024]{3,2,1,0:T(8,128)(2,1)}, u32[]{:S(2)}, u32[]{:S(2)}) %all-to-all-start.5) | async-done | bytes 8388640 | tf_op jit(solution)/shard_map/all_to_all | solution.py:135
  561.7 19.2 %multiply_convert_fusion = bf16[32,2,8,64,128]{4,3,2,1,0:T(8,128)(2,1)} fusion(f32[32,2,8,64,128]{4,3,2,1,0:T(8,128)} %get-tuple-element.19, bf16[32,2,128,8,128]{2,4,3,1,0:T(8,128)(2,1)} %bitcast.237, f32[32,2,8,64]{3,2,1,0:T(8,128)S(1)} %reshape.341, f32[32,2,8,64]{3,2,1,0:T(8,128)S(1)} %reshape.343, bf16[32,2,64,1024]{3,2,1,0:T(8,128)(2,1)} %all-to-all-done.5), kind=kOutput, calls=%fused_computation.14 | convolution fusion | flops 1098907648 | bytes 50593792 | tf_op jit(solution)/shard_map/abthd,abrhd->abhtr/dot_general | solution.py:150
  581.0 18.2 %convert_bitcast_fusion.1 = bf16[32,2,8,8,8,128]{5,4,3,2,1,0:T(8,128)(2,1)} fusion(bf16[32,2,128,8,128]{2,4,3,1,0:T(8,128)(2,1)} %bitcast.233, bf16[32,2,8,64,128]{4,3,2,1,0:T(8,128)(2,1)} %multiply_convert_fusion), kind=kOutput, calls=%fused_computation.36 | convolution fusion | flops 1077936128 | bytes 33554432 | tf_op jit(solution)/shard_map/abhtr,abrhd->abthd/dot_general | solution.py:154
  599.2 9.0 %copy.300 = bf16[32,2,8,8,8,128]{5,4,2,3,1,0:T(8,128)(2,1)} copy(bf16[32,2,8,8,8,128]{5,4,3,2,1,0:T(8,128)(2,1)} %convert_bitcast_fusion.1) | data formatting | bytes 16777216 | tf_op jit(solution)/shard_map/reshape | solution.py:157
  608.2 20.6 %all-to-all-start.7 = ((bf16[32,2,64,1024]{3,2,1,0:T(8,128)(2,1)}), bf16[32,2,64,1024]{3,2,1,0:T(8,128)(2,1)}, u32[]{:S(2)}, u32[]{:S(2)}) async-start(bf16[32,2,64,1024]{3,2,1,0:T(8,128)(2,1)} %bitcast.239), calls=%async_computation.7 | async-start | bytes 16777216 | tf_op jit(solution)/shard_map/all_to_all | solution.py:158
  628.9 9.0 %copy_bitcast_fusion.3 = bf16[32,2,64,8,128]{4,2,1,0,3:T(8,128)(2,1)} fusion(bf16[32,2,64,1024]{3,2,1,0:T(8,128)(2,1)} %all-to-all-done), kind=kLoop, calls=%fused_computation.24 | loop fusion | bytes 16777216 | tf_op jit(solution)/shard_map/reshape | solution.py:20
  637.9 9.0 %copy_bitcast_fusion.2 = bf16[32,2,64,8,128]{4,2,1,0,3:T(8,128)(2,1)} fusion(bf16[32,2,64,1024]{3,2,1,0:T(8,128)(2,1)} %all-to-all-done.5), kind=kLoop, calls=%fused_computation.23 | loop fusion | bytes 16777216 | tf_op jit(solution)/shard_map/reshape | solution.py:20
  647.0 13.8 %fusion.53 = bf16[2,128,8,128]{1,3,0,2:T(8,128)(2,1)S(1)} fusion(bf16[32,2,64,8,128]{4,2,1,0,3:T(8,128)(2,1)} %copy_bitcast_fusion.2, bf16[32,2,2]{1,0,2:T(8,128)(2,1)S(1)} %fusion.69, f32[32,2,8,64,128]{4,3,2,1,0:T(8,128)} %get-tuple-element.19, f32[32,2,8,64]{3,2,1,0:T(8,128)S(1)} %reshape.343), kind=kOutput, calls=%fused_computation.70 | convolution fusion | flops 2168717312 | bytes 25821440 | tf_op jit(solution)/shard_map/abhtr,abnthd->nrhd/dot_general | solution.py:166
  674.7 10.0 %fusion.48 = bf16[2,128,8,128]{1,3,0,2:T(8,128)(2,1)S(1)} fusion(bf16[32,2,2]{1,0,2:T(8,128)(2,1)S(1)} %fusion.69, bf16[32,2,64,8,128]{4,2,1,0,3:T(8,128)(2,1)} %copy_bitcast_fusion.3, bf16[32,2,8,64,128]{4,3,2,1,0:T(8,128)(2,1)} %multiply_convert_fusion), kind=kOutput, calls=%fused_computation.69 | convolution fusion | flops 2156134400 | bytes 17301760 | tf_op jit(solution)/shard_map/abhtr,abnthd->nrhd/dot_general | solution.py:162
  690.8 7.8 fusion.21
  698.7 38.7 %all-to-all-done.7 = bf16[32,2,64,1024]{3,2,1,0:T(8,128)(2,1)} async-done(((bf16[32,2,64,1024]{3,2,1,0:T(8,128)(2,1)}), bf16[32,2,64,1024]{3,2,1,0:T(8,128)(2,1)}, u32[]{:S(2)}, u32[]{:S(2)}) %all-to-all-start.7) | async-done | bytes 8388640 | tf_op jit(solution)/shard_map/all_to_all | solution.py:158
  737.4 12.0 %copy.244 = bf16[8,8,64,1024]{3,1,2,0:T(8,128)(2,1)} copy(bf16[8,8,64,1024]{3,2,1,0:T(8,128)(2,1)} %bitcast.96) | data formatting | bytes 16777216
  749.3 12.7 %gather_fusion.4 = bf16[28,65536]{1,0:T(8,128)(2,1)} fusion(bf16[64,65536]{1,0:T(8,128)(2,1)} %bitcast.234, s32[1024]{0:T(1024)} %copy-done.5), kind=kCustom, calls=%fused_computation.1.clone | custom fusion | bytes 7340144 | tf_op jit(solution)/shard_map/jit(_take)/gather | solution.py:179
  773.9 8.2 fusion.78
  792.3 19.2 %collective-permute-start.2 = (bf16[63,1024]{1,0:T(8,128)(2,1)S(1)}, bf16[63,1024]{1,0:T(8,128)(2,1)S(1)}, u32[]{:S(2)}, u32[]{:S(2)}) collective-permute-start(bf16[63,1024]{1,0:T(8,128)(2,1)S(1)} %slice.94), channel_id=1, source_target_pairs={{0,1},{1,2},{2,3},{3,4},{4,5},{5,6},{6,7},{7,8},{8,9},{9,10},{10,1... | collective-permute-start | bytes 387080 | tf_op jit(solution)/shard_map/ppermute | solution.py:16
  (138 shorter events, 149.4 us)
Async XLA Ops:
  7.2 56.0 %copy-start = (bf16[2,128,4096]{2,1,0:T(8,128)(2,1)S(1)}, bf16[2,128,4096]{2,1,0:T(8,128)(2,1)}, u32[]{:S(2)}) copy-start(bf16[2,128,4096]{2,1,0:T(8,128)(2,1)} %param.11) | copy-start | bytes 6291460
  9.4 400.2 %copy-start.6 = (pred[28]{0:T(512)(128)(4,1)}, pred[28]{0:T(512)(128)(4,1)S(1)}, u32[]{:S(2)}) copy-start(pred[28]{0:T(512)(128)(4,1)S(1)} %get-tuple-element.8) | copy-start | bytes 88
  10.2 43.2 %all-to-all-start.1 = ((bf16[32,1,2]{2,1,0:T(2,128)(2,1)}), bf16[32,1,2]{2,1,0:T(2,128)(2,1)S(1)}, u32[]{:S(2)}, u32[]{:S(2)}) async-start(bf16[32,1,2]{2,1,0:T(2,128)(2,1)} %convert_element_type.232), calls=%async_computation.1 | async-start | bytes 32768 | tf_op jit(solution)/shard_map/all_to_all | solution.py:91
  20.9 7.7 collective-permute-start
  53.5 118.3 %all-to-all-start = ((bf16[32,2,64,1024]{3,2,1,0:T(8,128)(2,1)}), bf16[32,2,64,1024]{3,2,1,0:T(8,128)(2,1)}, u32[]{:S(2)}, u32[]{:S(2)}) async-start(bf16[32,2,64,1024]{3,2,1,0:T(8,128)(2,1)} %bitcast.240), calls=%async_computation | async-start | bytes 16777216 | tf_op jit(solution)/shard_map/all_to_all | solution.py:90
  74.7 7.6 copy-start.8
  198.1 48.9 %all-to-all-start.2 = ((f32[32,1,1024]{2,1,0:T(1,128)}), f32[32,1,1024]{2,1,0:T(1,128)S(1)}, u32[]{:S(2)}, u32[]{:S(2)}) async-start(f32[32,1,1024]{2,1,0:T(1,128)} %reshape.338), calls=%async_computation.2 | async-start | bytes 262144 | tf_op jit(solution)/shard_map/all_to_all | solution.py:108
  247.0 9.6 %copy-start.4 = (s32[14,2]{0,1:T(2,128)S(1)}, s32[14,2]{0,1:T(2,128)}, u32[]{:S(2)}) copy-start(s32[14,2]{0,1:T(2,128)} %param.14) | copy-start | bytes 340
  247.0 116.1 %all-to-all-start.3 = ((bf16[32,2,64,1024]{3,2,1,0:T(8,128)(2,1)}), bf16[32,2,64,1024]{3,2,1,0:T(8,128)(2,1)}, u32[]{:S(2)}, u32[]{:S(2)}) async-start(bf16[32,2,64,1024]{3,2,1,0:T(8,128)(2,1)} %bitcast.238), calls=%async_computation.3 | async-start | bytes 16777216 | tf_op jit(solution)/shard_map/all_to_all | solution.py:105
  257.0 139.7 %copy-start.5 = (s32[1024]{0:T(1024)}, s32[1024]{0:T(1024)S(1)}, u32[]{:S(2)}) copy-start(s32[1024]{0:T(1024)S(1)} %pad_clamp_fusion) | copy-start | bytes 12292
  363.1 57.5 %all-to-all-start.4 = ((f32[32,1,1024]{2,1,0:T(1,128)}), f32[32,1,1024]{2,1,0:T(1,128)}, u32[]{:S(2)}, u32[]{:S(2)}) async-start(f32[32,1,1024]{2,1,0:T(1,128)} %reshape.342), calls=%async_computation.4 | async-start | bytes 262144 | tf_op jit(solution)/shard_map/all_to_all | solution.py:138
  412.2 3.2 copy-start.3
  413.6 1.8 copy-start.2
  420.6 24.6 %all-to-all-start.6 = ((f32[32,1,1024]{2,1,0:T(1,128)}), f32[32,1,1024]{2,1,0:T(1,128)S(1)}, u32[]{:S(2)}, u32[]{:S(2)}) async-start(f32[32,1,1024]{2,1,0:T(1,128)} %reshape.340), calls=%async_computation.6 | async-start | bytes 262144 | tf_op jit(solution)/shard_map/all_to_all | solution.py:139
  445.2 7.9 copy-start.9
  445.2 116.5 %all-to-all-start.5 = ((bf16[32,2,64,1024]{3,2,1,0:T(8,128)(2,1)}), bf16[32,2,64,1024]{3,2,1,0:T(8,128)(2,1)}, u32[]{:S(2)}, u32[]{:S(2)}) async-start(bf16[32,2,64,1024]{3,2,1,0:T(8,128)(2,1)} %bitcast.241), calls=%async_computation.5 | async-start | bytes 16777216 | tf_op jit(solution)/shard_map/all_to_all | solution.py:135
  608.2 129.2 %all-to-all-start.7 = ((bf16[32,2,64,1024]{3,2,1,0:T(8,128)(2,1)}), bf16[32,2,64,1024]{3,2,1,0:T(8,128)(2,1)}, u32[]{:S(2)}, u32[]{:S(2)}) async-start(bf16[32,2,64,1024]{3,2,1,0:T(8,128)(2,1)} %bitcast.239), calls=%async_computation.7 | async-start | bytes 16777216 | tf_op jit(solution)/shard_map/all_to_all | solution.py:158
  628.8 187.5 %reduce-scatter.2.cloned.1.call-start = ((), (), s32[]{:S(2)}) async-start(), calls=%async_computation.9 | async-start | bytes 5242880 | tf_op jit(solution)/shard_map/reduce_scatter | solution.py:172
  671.2 140.3 %collective-permute-start.1 = (bf16[63,1024]{1,0:T(8,128)(2,1)S(1)}, bf16[63,1024]{1,0:T(8,128)(2,1)S(1)}, u32[]{:S(2)}, u32[]{:S(2)}) collective-permute-start(bf16[63,1024]{1,0:T(8,128)(2,1)S(1)} %slice.89), channel_id=1, source_target_pairs={{0,1},{1,2},{2,3},{3,4},{4,5},{5,6},{6,7},{7,8},{8,9},{9,10},{10,1... | collective-permute-start | bytes 387080 | tf_op jit(solution)/shard_map/ppermute | solution.py:16
  749.3 12.7 %copy-start.7 = (pred[28]{0:T(512)(128)(4,1)S(1)}, pred[28]{0:T(512)(128)(4,1)}, u32[]{:S(2)}) copy-start(pred[28]{0:T(512)(128)(4,1)} %copy-done.6) | copy-start | bytes 88
  782.1 36.3 %copy-start.1 = (bf16[2,128,4096]{2,1,0:T(8,128)(2,1)S(1)}, bf16[2,128,4096]{2,1,0:T(8,128)(2,1)}, u32[]{:S(2)}) copy-start(bf16[2,128,4096]{2,1,0:T(8,128)(2,1)} %param.11) | copy-start | bytes 6291460
  791.2 23.5 %slice-start = ((bf16[896,1024]{1,0:T(8,128)(2,1)}), bf16[833,1024]{1,0:T(8,128)(2,1)S(1)}, s32[]{:S(2)}) async-start(bf16[896,1024]{1,0:T(8,128)(2,1)} %convert_element_type.211), calls=%async_computation.10 | async-start | bytes 3440640 | tf_op jit(solution)/shard_map/slice | solution.py:189
  792.3 22.4 %collective-permute-start.2 = (bf16[63,1024]{1,0:T(8,128)(2,1)S(1)}, bf16[63,1024]{1,0:T(8,128)(2,1)S(1)}, u32[]{:S(2)}, u32[]{:S(2)}) collective-permute-start(bf16[63,1024]{1,0:T(8,128)(2,1)S(1)} %slice.94), channel_id=1, source_target_pairs={{0,1},{1,2},{2,3},{3,4},{4,5},{5,6},{6,7},{7,8},{8,9},{9,10},{10,1... | collective-permute-start | bytes 387080 | tf_op jit(solution)/shard_map/ppermute | solution.py:16
Sparse Core Ops, SparseCore 0:
  698.8 47.1 reduce-scatter.1
where the time goes:
time: 836 us; the launch traced here: 826 us
  waiting for transfers between devices  279 us (33%)
  local copies, waits for them, and re-layouts  218 us (26%)
  matrix products  133 us (16%)
  starting transfers between devices  130 us (16%)
  other arithmetic  50.5 us (6%)
  between operations  14.8 us (2%)
    all_to_all x1, waiting for transfers between devices, per_device(): lax.all_to_all(grad_slots.astype(jnp.float32), 'seq', split_axis=0, conca...  106 us
    all_to_all x1, waiting for transfers between devices, per_device(): lax.all_to_all(part_out.astype(jnp.float32), 'seq', split_axis=0, concat_...  94.7 us
    unnamed x35, local copies, waits for them, and re-layouts  57.6 us
    all_to_all x1, waiting for transfers between devices, per_device(): lax.all_to_all(query_part, 'seq', split_axis=0, concat_axis=0, tiled=True)  38.7 us
    all_to_all x1, waiting for transfers between devices, per_device(): lax.all_to_all(query_slots, 'seq', split_axis=0, concat_axis=0, tiled=True)  38.5 us
    gather x2, local copies, waits for them, and re-layouts, per_device(): value_table[wanted]  29.2 us
    gather x2, local copies, waits for them, and re-layouts, per_device(): slot_score = slot_scores(asked_rows, key_table[wanted], head_count)  29.2 us
    ppermute x3, starting transfers between devices, shifted(): lax.ppermute(value, axis, [(source, source + steps) for source in range(f...  24.9 us
  transfers between devices with their start and end apart: 12, of which 5 were waited for; matrix products, arithmetic and copies ran while one was open for 39% of the time, Pallas kernels for 0%

commit v1 on v0

v1 whole, which is shorter than its diff:
```python
import math

import jax
import jax.numpy as jnp
from jax import lax
from jax.experimental import pallas as pl
from jax.experimental.pallas import tpu as pltpu
from jax.sharding import PartitionSpec as P

HD = 128
SPAN = 64
NBR_LEN = 128
MESH = pl.DeviceIdType.MESH
SCALE = 1.0 / math.sqrt(HD)
RING = 4
MIB = 1024 * 1024


def place():
    s = lax.axis_index("seq")
    return lax.div(s, 8), lax.rem(lax.div(s, 2), RING), lax.rem(s, 2)


def up(i):
    return lax.rem(i + 1, RING)


def down(i):
    return lax.rem(i + RING - 1, RING)


def across(i):
    return lax.rem(i + 2, RING)


def index_of(y, z, c):
    return y * 8 + z * 2 + c


def greet(y, z, c):
    barrier = pltpu.get_barrier_semaphore()
    for other in (
        index_of(up(y), z, c),
        index_of(down(y), z, c),
        index_of(y, up(z), c),
        index_of(y, down(z), c),
        index_of(y, z, 1 - c),
    ):
        pl.semaphore_signal(barrier, inc=1, device_id={"seq": other}, device_id_type=MESH)
    pl.semaphore_wait(barrier, 5)


def gather_kernel(own, tab, send_sem, recv_sem, own_sem):
    y, z, c = place()
    greet(y, z, c)
    pairs = own.shape[0] // 2

    def head_ops(h, parity):
        f, g = (y, z) if parity == 0 else (z, y)

        def dev(a, b):
            return index_of(a, b, c) if parity == 0 else index_of(b, a, c)

        def block(a, *half):
            return tab.at[(h, a, g, c) + half] if parity == 0 else tab.at[(h, g, a, c) + half]

        def band(b, *half):
            if parity == 0:
                return tab.at[(h, slice(None), b, c) + half]
            return tab.at[(h, b, slice(None), c) + half]

        def remote(kind, src, dst, to):
            return pltpu.make_async_remote_copy(
                src_ref=src,
                dst_ref=dst,
                send_sem=send_sem.at[h, kind],
                recv_sem=recv_sem.at[h, kind],
                device_id={"seq": to},
                device_id_type=MESH,
            )

        sibling = index_of(y, z, 1 - c)
        mine = pltpu.make_async_copy(own.at[h], block(f), own_sem.at[h])
        moves = [
            remote(0, own.at[h], block(f), dev(up(f), g)),
            remote(1, own.at[h], block(f), dev(down(f), g)),
            remote(2, block(down(f), 0), block(down(f), 0), dev(up(f), g)),
            remote(3, block(up(f), 1), block(up(f), 1), dev(down(f), g)),
            remote(4, band(g), band(g), dev(f, up(g))),
            remote(5, band(g), band(g), dev(f, down(g))),
            remote(6, band(down(g), slice(0, 1)), band(down(g), slice(0, 1)), dev(f, up(g))),
            remote(7, band(up(g), slice(1, 2)), band(up(g), slice(1, 2)), dev(f, down(g))),
            remote(8, band(g), band(g), sibling),
            remote(9, band(down(g)), band(down(g)), sibling),
            remote(10, band(up(g)), band(up(g)), sibling),
            remote(11, band(across(g)), band(across(g)), sibling),
        ]
        return mine, moves

    def stage0(mine, moves):
        mine.start()
        moves[0].start()
        moves[1].start()

    def stage1(mine, moves):
        moves[0].wait_recv()
        moves[2].start()
        moves[1].wait_recv()
        moves[3].start()

    def stage2(mine, moves):
        mine.wait()
        moves[2].wait_recv()
        moves[3].wait_recv()
        moves[4].start()
        moves[5].start()
        moves[8].start()

    def stage3(mine, moves):
        moves[4].wait_recv()
        moves[6].start()
        moves[9].start()
        moves[5].wait_recv()
        moves[7].start()
        moves[10].start()

    def stage4(mine, moves):
        moves[6].wait_recv()
        moves[7].wait_recv()
        moves[11].start()

    def stage5(mine, moves):
        for kind in (8, 9, 10, 11):
            moves[kind].wait_recv()
        for move in moves:
            move.wait_send()

    stages = (stage0, stage1, stage2, stage3, stage4, stage5)

    def step(i, carry):
        for lag, stage in enumerate(stages):

            @pl.when((i >= lag) & (i < pairs + lag))
            def _(lag=lag, stage=stage):
                for parity in (0, 1):
                    stage(*head_ops(2 * (i - lag) + parity, parity))

        return carry

    lax.fori_loop(0, pairs + len(stages) - 1, step, 0)


def gather_tables(own):
    heads = own.shape[0]
    return pl.pallas_call(
        gather_kernel,
        out_shape=jax.ShapeDtypeStruct((heads, RING, RING, 2) + own.shape[1:], own.dtype),
        in_specs=[pl.BlockSpec(memory_space=pl.ANY)],
        out_specs=pl.BlockSpec(memory_space=pl.ANY),
        scratch_shapes=[
            pltpu.SemaphoreType.DMA((heads, 12)),
            pltpu.SemaphoreType.DMA((heads, 12)),
            pltpu.SemaphoreType.DMA((heads,)),
        ],
        compiler_params=pltpu.CompilerParams(collective_id=0, has_side_effects=True),
        name="gather_tables",
    )(own)


def dot_t(a, b):
    return lax.dot_general(a, b, (((1,), (1,)), ((), ())), preferred_element_type=jnp.float32)


def t_dot(a, b):
    return lax.dot_general(a, b, (((0,), (0,)), ((), ())), preferred_element_type=jnp.float32)


def span_math(q, g, keys, values):
    exps, tops, sums, outs = [], [], [], []
    for k, v in zip(keys, values):
        s = dot_t(q, k) * SCALE
        top = jnp.max(s, axis=1, keepdims=True)
        e = jnp.exp(s - top)
        total = jnp.sum(e, axis=1, keepdims=True)
        p = (e * (1.0 / total)).astype(jnp.bfloat16)
        out = jnp.dot(p, v, preferred_element_type=jnp.float32)
        exps.append(e)
        tops.append(top)
        sums.append(total)
        outs.append(out.astype(jnp.bfloat16).astype(jnp.float32))
    top = jnp.maximum(tops[0], tops[1])
    lifts = [jnp.exp(t - top) for t in tops]
    inverse = 1.0 / (sums[0] * lifts[0] + sums[1] * lifts[1])
    shares = [sums[j] * lifts[j] * inverse for j in (0, 1)]
    merged = shares[0] * outs[0] + shares[1] * outs[1]
    delta = jnp.sum(g.astype(jnp.float32) * merged, axis=1, keepdims=True)
    d_query, d_keys, d_values = 0.0, [], []
    for j in (0, 1):
        full = exps[j] * (lifts[j] * inverse)
        grad = dot_t(g, values[j])
        ds = (full * (grad - delta) * SCALE).astype(jnp.bfloat16)
        part = jnp.dot(ds, keys[j], preferred_element_type=jnp.float32)
        d_query = d_query + part.astype(jnp.bfloat16).astype(jnp.float32)
        d_keys.append(t_dot(ds, q))
        d_values.append(t_dot(full.astype(jnp.bfloat16), g))
    return merged, d_query, d_keys, d_values


def attend_kernel(ids, first, second, q_ref, g_ref, tab, att_ref, dq_ref, con, ck, cv):
    spans = q_ref.shape[0] // SPAN
    reads = 2 * spans
    ck[reads] = jnp.zeros(ck.shape[1:], jnp.float32)
    cv[reads] = jnp.zeros(cv.shape[1:], jnp.float32)

    def one(c, carry):
        rows = pl.ds(pl.multiple_of(c * SPAN, SPAN), SPAN)
        q, g = q_ref[rows, :], g_ref[rows, :]
        picks = [ids[2 * c + j] for j in (0, 1)]
        spots = [(lax.div(n, 2), lax.rem(n, 2)) for n in picks]
        keys = [tab[0, o, 0, s] for o, s in spots]
        values = [tab[0, o, 1, s] for o, s in spots]
        merged, d_query, d_keys, d_values = span_math(q, g, keys, values)
        att_ref[rows, :] = merged.astype(jnp.bfloat16)
        dq_ref[rows, :] = d_query.astype(jnp.bfloat16)
        for j in (0, 1):
            ck[2 * c + j] = d_keys[j]
            cv[2 * c + j] = d_values[j]
        return carry

    lax.fori_loop(0, spans, one, 0, unroll=2)

    def fold(o, carry):
        for s in (0, 1):
            a, b = first[2 * o + s], second[2 * o + s]
            con[0, o, 0, s] = (ck[a] + ck[b]).astype(jnp.bfloat16)
            con[0, o, 1, s] = (cv[a] + cv[b]).astype(jnp.bfloat16)
        return carry

    lax.fori_loop(0, tab.shape[1], fold, 0)


def attend(ids, first, second, query_shift, grad_shift, tables):
    rows, width = query_shift.shape
    heads, owners = tables.shape[0], tables.shape[1]
    reads = ids.shape[0]
    row_spec = pl.BlockSpec((rows, HD), lambda h, *_: (0, h))
    tab_spec = pl.BlockSpec((1,) + tables.shape[1:], lambda h, *_: (h, 0, 0, 0, 0, 0))
    return pl.pallas_call(
        attend_kernel,
        grid_spec=pltpu.PrefetchScalarGridSpec(
            num_scalar_prefetch=3,
            grid=(heads,),
            in_specs=[row_spec, row_spec, tab_spec],
            out_specs=[row_spec, row_spec, tab_spec],
            scratch_shapes=[
                pltpu.VMEM((reads + 1, NBR_LEN, HD), jnp.float32),
                pltpu.VMEM((reads + 1, NBR_LEN, HD), jnp.float32),
            ],
        ),
        out_shape=[
            jax.ShapeDtypeStruct((rows, width), jnp.bfloat16),
            jax.ShapeDtypeStruct((rows, width), jnp.bfloat16),
            jax.ShapeDtypeStruct(tables.shape, jnp.bfloat16),
        ],
        compiler_params=pltpu.CompilerParams(vmem_limit_bytes=48 * MIB),
        name="attend",
    )(ids, first, second, query_shift, grad_shift, tables)


def wide(value):
    return value.astype(jnp.float32)


def scatter_kernel(con, out, acc, sib, r1, r2, r3, r4, send_sem, recv_sem, own_sem):
    y, z, c = place()
    greet(y, z, c)
    pairs = out.shape[0] // 2

    def head_ops(h, parity):
        f, g = (y, z) if parity == 0 else (z, y)

        def dev(a, b):
            return index_of(a, b, c) if parity == 0 else index_of(b, a, c)

        def spot(a, b):
            return (h, a, b) if parity == 0 else (h, b, a)

        def remote(kind, src, dst, to):
            return pltpu.make_async_remote_copy(
                src_ref=src,
                dst_ref=dst,
                send_sem=send_sem.at[h, kind],
                recv_sem=recv_sem.at[h, kind],
                device_id={"seq": to},
                device_id_type=MESH,
            )

        every = slice(None)
        mine = pltpu.make_async_copy(con.at[h, :, :, c], acc.at[h], own_sem.at[h])
        moves = [
            remote(0, con.at[h, :, :, 1 - c], sib.at[h], index_of(y, z, 1 - c)),
            remote(1, acc.at[spot(every, across(g)) + (0,)], r1.at[h, 0], dev(f, up(g))),
            remote(2, acc.at[spot(every, across(g)) + (1,)], r1.at[h, 1], dev(f, down(g))),
            remote(3, acc.at[spot(every, up(g))], r2.at[h, 0], dev(f, up(g))),
            remote(4, acc.at[spot(every, down(g))], r2.at[h, 1], dev(f, down(g))),
            remote(5, acc.at[spot(across(f), g) + (0,)], r3.at[h, 0], dev(up(f), g)),
            remote(6, acc.at[spot(across(f), g) + (1,)], r3.at[h, 1], dev(down(f), g)),
            remote(7, acc.at[spot(up(f), g)], r4.at[h, 0], dev(up(f), g)),
            remote(8, acc.at[spot(down(f), g)], r4.at[h, 1], dev(down(f), g)),
        ]
        return h, spot, f, g, mine, moves

    def stage0(h, spot, f, g, mine, moves):
        mine.start()
        moves[0].start()

    def stage1(h, spot, f, g, mine, moves):
        mine.wait()
        moves[0].wait_recv()

        def add(i, carry):
            a, b = lax.div(i, RING), lax.rem(i, RING)
            for kv in (0, 1):
                acc[h, a, b, kv] = acc[h, a, b, kv] + sib[h, a, b, kv]
            return carry

        lax.fori_loop(0, RING * RING, add, 0)
        moves[1].start()
        moves[2].start()

    def stage2(h, spot, f, g, mine, moves):
        for half, (move, toward) in enumerate(((1, up(g)), (2, down(g)))):
            moves[move].wait_recv()

            def add(a, carry):
                at = spot(a, toward) + (half,)
                acc[at] = acc[at] + r1[h, half, a]
                return carry

            lax.fori_loop(0, RING, add, 0)
            moves[3 + half].start()

    def stage3(h, spot, f, g, mine, moves):
        moves[3].wait_recv()
        moves[4].wait_recv()

        def add(a, carry):
            for kv in (0, 1):
                at = spot(a, g) + (kv,)
                total = wide(acc[at]) + wide(r2[h, 0, a, kv]) + wide(r2[h, 1, a, kv])
                acc[at] = total.astype(jnp.bfloat16)
            return carry

        lax.fori_loop(0, RING, add, 0)
        moves[5].start()
        moves[6].start()

    def stage4(h, spot, f, g, mine, moves):
        for half, (move, toward) in enumerate(((5, up(f)), (6, down(f)))):
            moves[move].wait_recv()
            at = spot(toward, g) + (half,)
            acc[at] = acc[at] + r3[h, half]
            moves[7 + half].start()

    def stage5(h, spot, f, g, mine, moves):
        moves[7].wait_recv()
        moves[8].wait_recv()
        for kv in (0, 1):
            total = wide(acc[spot(f, g) + (kv,)]) + wide(r4[h, 0, kv]) + wide(r4[h, 1, kv])
            out[h, kv] = total.astype(jnp.bfloat16)
        for move in moves:
            move.wait_send()

    stages = (stage0, stage1, stage2, stage3, stage4, stage5)

    def step(i, carry):
        for lag, stage in enumerate(stages):

            @pl.when((i >= lag) & (i < pairs + lag))
            def _(lag=lag, stage=stage):
                for parity in (0, 1):
                    stage(*head_ops(2 * (i - lag) + parity, parity))

        return carry

    lax.fori_loop(0, pairs + len(stages) - 1, step, 0)


def scatter_tables(con):
    heads = con.shape[0]
    tail = con.shape[5:]
    return pl.pallas_call(
        scatter_kernel,
        out_shape=jax.ShapeDtypeStruct((heads, 2) + tail, con.dtype),
        in_specs=[pl.BlockSpec(memory_space=pl.ANY)],
        out_specs=pl.BlockSpec(memory_space=pltpu.VMEM),
        scratch_shapes=[
            pltpu.VMEM((heads, RING, RING, 2) + tail, con.dtype),
            pltpu.VMEM((heads, RING, RING, 2) + tail, con.dtype),
            pltpu.VMEM((heads, 2, RING) + tail, con.dtype),
            pltpu.VMEM((heads, 2, RING, 2) + tail, con.dtype),
            pltpu.VMEM((heads, 2) + tail, con.dtype),
            pltpu.VMEM((heads, 2, 2) + tail, con.dtype),
            pltpu.SemaphoreType.DMA((heads, 9)),
            pltpu.SemaphoreType.DMA((heads, 9)),
            pltpu.SemaphoreType.DMA((heads,)),
        ],
        compiler_params=pltpu.CompilerParams(
            collective_id=1, has_side_effects=True, vmem_limit_bytes=56 * MIB
        ),
        name="scatter_tables",
    )(con)


def enc_kernel(part, out, s1, s2, r1, r2, send_sem, recv_sem):
    x = lax.axis_index("enc")
    right, left = up(x), down(x)
    barrier = pltpu.get_barrier_semaphore()
    for other in (right, left):
        pl.semaphore_signal(barrier, inc=1, device_id={"enc": other}, device_id_type=MESH)
    pl.semaphore_wait(barrier, 2)
    rows = part.shape[0]
    half = rows // 2
    width = out.shape[1]

    def cols(t):
        return pl.ds(pl.multiple_of(t * width, width), width)

    def remote(kind, src, dst, to):
        return pltpu.make_async_remote_copy(
            src_ref=src,
            dst_ref=dst,
            send_sem=send_sem.at[kind],
            recv_sem=recv_sem.at[kind],
            device_id={"enc": to},
            device_id_type=MESH,
        )

    moves = [
        remote(0, s1.at[0], r1.at[0], right),
        remote(1, s1.at[1], r1.at[1], left),
        remote(2, s2.at[0], r2.at[0], right),
        remote(3, s2.at[1], r2.at[1], left),
    ]
    far = cols(across(x))
    s1[0] = part[:half, far].astype(jnp.bfloat16)
    moves[0].start()
    s1[1] = part[half:, far].astype(jnp.bfloat16)
    moves[1].start()
    s2[0, half:] = part[half:, cols(right)].astype(jnp.bfloat16)
    s2[1, :half] = part[:half, cols(left)].astype(jnp.bfloat16)
    moves[0].wait_recv()
    s2[0, :half] = (part[:half, cols(right)] + wide(r1[0])).astype(jnp.bfloat16)
    moves[2].start()
    moves[1].wait_recv()
    s2[1, half:] = (part[half:, cols(left)] + wide(r1[1])).astype(jnp.bfloat16)
    moves[3].start()
    moves[2].wait_recv()
    moves[3].wait_recv()
    out[...] = (part[:, cols(x)] + wide(r2[0]) + wide(r2[1])).astype(jnp.bfloat16)
    for move in moves:
        move.wait_send()


def scatter_enc(part):
    rows, width = part.shape[0], part.shape[1] // RING
    half = rows // 2
    return pl.pallas_call(
        enc_kernel,
        out_shape=jax.ShapeDtypeStruct((rows, width), jnp.bfloat16),
        in_specs=[pl.BlockSpec(memory_space=pltpu.VMEM)],
        out_specs=pl.BlockSpec(memory_space=pltpu.VMEM),
        scratch_shapes=[
            pltpu.VMEM((2, half, width), jnp.bfloat16),
            pltpu.VMEM((2, rows, width), jnp.bfloat16),
            pltpu.VMEM((2, half, width), jnp.bfloat16),
            pltpu.VMEM((2, rows, width), jnp.bfloat16),
            pltpu.SemaphoreType.DMA((4,)),
            pltpu.SemaphoreType.DMA((4,)),
        ],
        compiler_params=pltpu.CompilerParams(
            collective_id=2, has_side_effects=True, vmem_limit_bytes=32 * MIB
        ),
        name="scatter_enc",
    )(part)


def shifted(value, axis, steps):
    count = lax.axis_size(axis)
    first, last = (max(0, -steps), min(count, count - steps))
    return lax.ppermute(value, axis, [(source, source + steps) for source in range(first, last)])


def per_device(queries, d_attended, encodings, w_key, w_value, neighbour_owner, neighbour_slot):
    tok_rows, feat_width = queries.shape
    heads = feat_width // HD
    margin = SPAN - 1
    owned = encodings.shape[0]
    owners = lax.axis_size("seq")
    reads = 2 * (tok_rows // SPAN)

    ids = (neighbour_owner * owned + neighbour_slot).reshape(reads).astype(jnp.int32)
    hit = ids[None, :] == jnp.arange(owners * owned, dtype=jnp.int32)[:, None]
    order = jnp.arange(reads, dtype=jnp.int32)[None, :]
    first = jnp.min(jnp.where(hit, order, reads), axis=1)
    last = jnp.max(jnp.where(hit, order, -1), axis=1)
    second = jnp.where(last > first, last, reads)

    rim_rows = shifted(jnp.stack([queries[:margin], d_attended[:margin]]), "seq", -1)
    query_shift = jnp.concatenate([queries[margin:], rim_rows[0]], axis=0)
    grad_shift = jnp.concatenate([d_attended[margin:], rim_rows[1]], axis=0)

    enc_flat = encodings.reshape(owned * NBR_LEN, encodings.shape[2])
    tables = [
        jnp.dot(enc_flat, w, preferred_element_type=jnp.float32)
        .astype(jnp.bfloat16)
        .reshape(owned * NBR_LEN, heads, HD)
        .transpose(1, 0, 2)
        for w in (w_key, w_value)
    ]
    table = gather_tables(jnp.stack(tables, axis=1))
    table = table.reshape(heads, owners, 2, owned, NBR_LEN, HD)
    attended_shift, dq_shift, con = attend(ids, first, second, query_shift, grad_shift, table)
    attended_tail = shifted(attended_shift[tok_rows - margin :], "seq", 1)
    query_tail = shifted(dq_shift[tok_rows - margin :], "seq", 1)
    con = con.reshape(heads, RING, RING, 2, 2, owned * NBR_LEN, HD)
    grads = scatter_tables(con)
    contract = (((1,), (1,)), ((), ()))
    part = 0.0
    for kv, w in enumerate((w_key, w_value)):
        rows = grads[:, kv].transpose(1, 0, 2).reshape(owned * NBR_LEN, feat_width)
        part = part + lax.dot_general(rows, w, contract, preferred_element_type=jnp.float32)
    d_encodings = scatter_enc(part).reshape(owned, NBR_LEN, feat_width)
    attended = jnp.concatenate([attended_tail, attended_shift[: tok_rows - margin]], axis=0)
    d_queries = jnp.concatenate([query_tail, dq_shift[: tok_rows - margin]], axis=0)
    return (attended, d_queries, d_encodings)


def solution(mesh):
    return jax.shard_map(
        per_device,
        mesh=mesh,
        in_specs=(
            P("seq", "enc"),
            P("seq", "enc"),
            P("seq", None, None),
            P(None, "enc"),
            P(None, "enc"),
            P("seq", None),
            P("seq", None),
        ),
        out_specs=(P("seq", "enc"), P("seq", "enc"), P("seq", None, "enc")),
        check_vma=False,
    )
```

time: 836 us -> 417 us (0.50); the launches traced: 826 us -> 416 us
  Pallas kernels: 0 us -> 364 us
  waiting for transfers between devices: 279 us -> 0.01 us
  local copies, waits for them, and re-layouts: 218 us -> 11.2 us
  starting transfers between devices: 130 us -> 7.69 us
  matrix products: 133 us -> 23.1 us
  other arithmetic: 50.5 us -> 9.16 us
  between operations: 14.8 us -> 0.86 us
    pallas_call x0 -> x4, Pallas kernels: none -> 364 us  [the longest x1 147 us: attend(): pl.pallas_call(attend_kernel, grid_spec=pltpu.PrefetchScalarGridSpec(num_...]
    all_to_all x8 -> x0, waiting for transfers between devices: 278 us -> none  [the longest x1 106 us: per_device(): lax.all_to_all(grad_slots.astype(jnp.float32), 'seq', split_axis=0, conca...]
    dot_general x14 -> x4, matrix products: 133 us -> 23.1 us  [the longest x2 11.7 us: per_device(): lax.dot_general(rows, w, contract, preferred_element_type=jnp.float32)]
    all_to_all x8 -> x0, starting transfers between devices: 105 us -> none  [the longest x1 21.7 us: per_device(): lax.all_to_all(total_slots, 'seq', split_axis=0, concat_axis=0, tiled=True)]
    gather x8 -> x0, local copies, waits for them, and re-layouts: 84.5 us -> none  [the longest x2 29.2 us: per_device(): value_table[wanted]]
    unnamed x35 -> x11, local copies, waits for them, and re-layouts: 57.6 us -> 0.83 us
    reshape x9 -> x3, local copies, waits for them, and re-layouts: 40 us -> 0.65 us  [the longest x2 0.56 us: per_device(): tables = [jnp.dot(enc_flat, w, preferred_element_type=jnp.float32).astype...]
    ppermute x3, starting transfers between devices: 24.9 us -> 7.69 us  [shifted(): lax.ppermute(value, axis, [(source, source + steps) for source in range(f...]
  transfers between devices with their start and end apart: 12 -> 3, of which waited for: 5 -> 0; matrix products, arithmetic and copies ran while one was open for 39% -> 8% of each run, Pallas kernels for 0% -> 28%
where the time goes in v1:
time: 417 us; the launch traced here: 416 us
  Pallas kernels  364 us (87%)
  matrix products  23.1 us (6%)
  local copies, waits for them, and re-layouts  11.2 us (3%)
  other arithmetic  9.16 us (2%)
  starting transfers between devices  7.69 us (2%)
    pallas_call x1, Pallas kernels, attend(): pl.pallas_call(attend_kernel, grid_spec=pltpu.PrefetchScalarGridSpec(num_...  147 us
    pallas_call x1, Pallas kernels, scatter_tables(): pl.pallas_call(scatter_kernel, out_shape=jax.ShapeDtypeStruct((heads, 2)...  98.7 us
    pallas_call x1, Pallas kernels, gather_tables(): pl.pallas_call(gather_kernel, out_shape=jax.ShapeDtypeStruct((heads, RING...  97.2 us
    pallas_call x1, Pallas kernels, scatter_enc(): pl.pallas_call(enc_kernel, out_shape=jax.ShapeDtypeStruct((rows, width),...  21.2 us
    dot_general x2, matrix products, per_device(): lax.dot_general(rows, w, contract, preferred_element_type=jnp.float32)  11.7 us
    dot_general x2, matrix products, per_device(): jnp.dot(enc_flat, w, preferred_element_type=jnp.float32)  11.4 us
  transfers between devices with their start and end apart: 3, of which 0 were waited for; matrix products, arithmetic and copies ran while one was open for 8% of the time, Pallas kernels for 28%

profile of v1, /device:TPU:1, one launch (start us, length us, event | category | flops | bytes accessed | tf_op | source)
XLA Modules:
  0.0 415.7 jit_solution(13467344974325786629)
XLA Ops:
  0.6 1.1 slice_bitcast_fusion.4
  1.8 0.7 pad_maximum_fusion.5
  2.5 3.3 collective-permute-start
  5.8 0.7 multiply_add_fusion
  6.5 0.1 copy.18
  6.7 5.7 %convolution_convert_fusion = bf16[256,1024]{1,0:T(8,128)(2,1)S(1)} fusion(bf16[256,4096]{1,0:T(8,128)(2,1)S(1)} %bitcast.39, bf16[4096,1024]{1,0:T(8,128)(2,1)} %param.11), kind=kOutput, calls=%fused_computation.5 | convolution fusion | flops 2147745792 | bytes 11010048 | tf_op jit(solution)/shard_map/dot_general | solution.py:515
  12.5 0.2 copy.21
  12.7 0.3 copy.22
  13.0 5.7 %convolution_convert_fusion.1 = bf16[256,1024]{1,0:T(8,128)(2,1)S(1)} fusion(bf16[256,4096]{1,0:T(8,128)(2,1)S(1)} %bitcast.38, bf16[4096,1024]{1,0:T(8,128)(2,1)} %param.10), kind=kOutput, calls=%fused_computation.6 | convolution fusion | flops 2147745792 | bytes 11010048 | tf_op jit(solution)/shard_map/dot_general | solution.py:515
  18.7 0.2 copy.19
  18.9 0.3 copy.20
  19.2 1.1 pad_maximum_fusion.4.own
  20.3 3.2 slice.36
  23.5 0.4 slice.40
  24.0 97.2 %gather_tables.1 = bf16[8,4,4,2,2,256,128]{6,5,4,3,2,1,0:T(8,128)(2,1)} custom-call(bf16[8,2,256,128]{3,2,1,0:T(8,128)(2,1)} %pad_maximum_fusion.4.own), custom_call_target="tpu_custom_call" | custom-call | tf_op jit(solution)/shard_map/gather_tables/pallas_call | solution.py:155
  121.3 1.7 pad_maximum_fusion.q_ref
  123.0 1.5 pad_maximum_fusion.1.g_ref
  124.4 146.6 %attend.1 = (bf16[896,1024]{1,0:T(8,128)(2,1)S(1)}, bf16[896,1024]{1,0:T(8,128)(2,1)S(1)}, bf16[8,32,2,2,128,128]{5,4,3,2,1,0:T(8,128)(2,1)}) custom-call(s32[28]{0:T(128)S(1)} %reshape.34.ids, s32[64]{0:T(128)S(1)} %get-tuple-element.10.first, s32[64]{0:T(128)S(1)} %compare_select_fusion.second, bf16[896,1024]{1,0:T(8,128)(2,1)S(1)} %pad_maximum_fusion.q_ref, ...), custom_call_target="tpu_custom_call" | custom-call | tf_op jit(solution)/shard_map/attend/pallas_call | solution.py:248
  271.0 1.3 slice.43
  272.4 1.3 slice.45
  273.7 98.7 %scatter_tables.1 = bf16[8,2,256,128]{3,2,1,0:T(8,128)(2,1)} custom-call(bf16[8,4,4,2,2,256,128]{6,5,4,3,2,1,0:T(8,128)(2,1)} %bitcast.42), custom_call_target="tpu_custom_call" | custom-call | tf_op jit(solution)/shard_map/scatter_tables/pallas_call | solution.py:392
  372.4 1.3 slice_bitcast_fusion
  373.7 0.2 copy.24
  373.9 2.3 collective-permute-start.2
  376.2 2.1 collective-permute-start.1
  378.3 0.2 copy.23
  378.5 5.8 %fusion = f32[256,4096]{1,0:T(8,128)S(1)} fusion(bf16[256,1024]{0,1:T(8,128)(2,1)S(1)} %bitcast.48, bf16[4096,1024]{1,0:T(8,128)(2,1)} %param.10), kind=kOutput, calls=%fused_computation.20 | convolution fusion | flops 2147483648 | bytes 13107200 | tf_op jit(solution)/shard_map/dot_general | solution.py:532
  384.3 5.9 %convolution_add_fusion.part = f32[256,4096]{1,0:T(8,128)S(1)} fusion(f32[256,4096]{1,0:T(8,128)S(1)} %fusion, bf16[256,1024]{0,1:T(8,128)(2,1)S(1)} %bitcast.47, bf16[4096,1024]{1,0:T(8,128)(2,1)} %param.11), kind=kOutput, calls=%fused_computation | convolution fusion | flops 2148532224 | bytes 17301504 | tf_op jit(solution)/shard_map/dot_general | solution.py:532
  390.2 21.2 %scatter_enc.1 = bf16[256,1024]{1,0:T(8,128)(2,1)S(1)} custom-call(f32[256,4096]{1,0:T(8,128)S(1)} %convolution_add_fusion.part), custom_call_target="tpu_custom_call" | custom-call | tf_op jit(solution)/shard_map/scatter_enc/pallas_call | solution.py:468
  411.4 1.7 pad_maximum_fusion.3
  413.2 1.7 pad_maximum_fusion.2
  414.9 0.8 copy.26
  (19 shorter events, 0.3 us)
Async XLA Ops:
  0.6 6.1 %copy-start = (bf16[2,128,4096]{2,1,0:T(8,128)(2,1)S(1)}, bf16[2,128,4096]{2,1,0:T(8,128)(2,1)}, u32[]{:S(2)}) copy-start(bf16[2,128,4096]{2,1,0:T(8,128)(2,1)} %param.9) | copy-start | bytes 6291460
  2.5 118.7 %collective-permute-start = (bf16[2,63,1024]{2,1,0:T(8,128)(2,1)}, bf16[2,63,1024]{2,1,0:T(8,128)(2,1)S(1)}, u32[]{:S(2)}, u32[]{:S(2)}) collective-permute-start(bf16[2,63,1024]{2,1,0:T(8,128)(2,1)} %pad_maximum_fusion.5), channel_id=1, source_target_pairs={{1,0},{2,1},{3,2},{4,3},{5,4},{6,5},{7,6},{8,7},{9,8},{10,9},{11,1... | collective-permute-start | bytes 774152 | tf_op jit(solution)/shard_map/ppermute | solution.py:491
  20.2 3.3 copy-start.4
  373.9 37.5 %collective-permute-start.2 = (bf16[63,1024]{1,0:T(8,128)(2,1)S(1)}, bf16[63,1024]{1,0:T(8,128)(2,1)S(1)}, u32[]{:S(2)}, u32[]{:S(2)}) collective-permute-start(bf16[63,1024]{1,0:T(8,128)(2,1)S(1)} %slice.44), channel_id=1, source_target_pairs={{0,1},{1,2},{2,3},{3,4},{4,5},{5,6},{6,7},{7,8},{8,9},{9,10},{10,1... | collective-permute-start | bytes 387080 | tf_op jit(solution)/shard_map/ppermute | solution.py:491
  376.2 37.0 %collective-permute-start.1 = (bf16[63,1024]{1,0:T(8,128)(2,1)S(1)}, bf16[63,1024]{1,0:T(8,128)(2,1)S(1)}, u32[]{:S(2)}, u32[]{:S(2)}) collective-permute-start(bf16[63,1024]{1,0:T(8,128)(2,1)S(1)} %slice.42), channel_id=1, source_target_pairs={{0,1},{1,2},{2,3},{3,4},{4,5},{5,6},{6,7},{7,8},{8,9},{9,10},{10,1... | collective-permute-start | bytes 387080 | tf_op jit(solution)/shard_map/ppermute | solution.py:491
  390.2 21.2 %copy-start.3 = (bf16[833,1024]{1,0:T(8,128)(2,1)S(1)}, bf16[833,1024]{1,0:T(8,128)(2,1)}, u32[]{:S(2)}) copy-start(bf16[833,1024]{1,0:T(8,128)(2,1)} %slice.45) | copy-start | bytes 5117956
  411.4 1.7 copy-start.2
  411.4 4.2 %copy-start.1 = (bf16[2,128,4096]{2,1,0:T(8,128)(2,1)S(1)}, bf16[2,128,4096]{2,1,0:T(8,128)(2,1)}, u32[]{:S(2)}) copy-start(bf16[2,128,4096]{2,1,0:T(8,128)(2,1)} %param.9) | copy-start | bytes 6291460

commit v2 on v1

--- a/solution.py
+++ b/solution.py
@@ -175,59 +175,78 @@
     return lax.dot_general(a, b, (((0,), (0,)), ((), ())), preferred_element_type=jnp.float32)
 
 
-def span_math(q, g, keys, values):
-    exps, tops, sums, outs = [], [], [], []
-    for k, v in zip(keys, values):
-        s = dot_t(q, k) * SCALE
-        top = jnp.max(s, axis=1, keepdims=True)
-        e = jnp.exp(s - top)
-        total = jnp.sum(e, axis=1, keepdims=True)
-        p = (e * (1.0 / total)).astype(jnp.bfloat16)
-        out = jnp.dot(p, v, preferred_element_type=jnp.float32)
-        exps.append(e)
-        tops.append(top)
-        sums.append(total)
-        outs.append(out.astype(jnp.bfloat16).astype(jnp.float32))
-    top = jnp.maximum(tops[0], tops[1])
-    lifts = [jnp.exp(t - top) for t in tops]
-    inverse = 1.0 / (sums[0] * lifts[0] + sums[1] * lifts[1])
-    shares = [sums[j] * lifts[j] * inverse for j in (0, 1)]
-    merged = shares[0] * outs[0] + shares[1] * outs[1]
-    delta = jnp.sum(g.astype(jnp.float32) * merged, axis=1, keepdims=True)
-    d_query, d_keys, d_values = 0.0, [], []
-    for j in (0, 1):
-        full = exps[j] * (lifts[j] * inverse)
-        grad = dot_t(g, values[j])
-        ds = (full * (grad - delta) * SCALE).astype(jnp.bfloat16)
-        part = jnp.dot(ds, keys[j], preferred_element_type=jnp.float32)
-        d_query = d_query + part.astype(jnp.bfloat16).astype(jnp.float32)
-        d_keys.append(t_dot(ds, q))
-        d_values.append(t_dot(full.astype(jnp.bfloat16), g))
+def spans_math(qs, gs, keys, values):
+    each, both = range(len(qs)), (0, 1)
+
+    def pairs(rows, tables):
+        joined = [dot_t(rows[u], jnp.concatenate(tables[u], axis=0)) for u in each]
+        return [[x[:, :NBR_LEN], x[:, NBR_LEN:]] for x in joined]
+
+    def narrow(x):
+        return x.astype(jnp.bfloat16)
+
+    s = pairs(qs, keys)
+    grad = pairs(gs, values)
+    top = [[jnp.max(s[u][j], axis=1, keepdims=True) for j in both] for u in each]
+    e = [[jnp.exp((s[u][j] - top[u][j]) * SCALE) for j in both] for u in each]
+    total = [[jnp.sum(e[u][j], axis=1, keepdims=True) for j in both] for u in each]
+    p = [[narrow(e[u][j] * (1.0 / total[u][j])) for j in both] for u in each]
+    out = [
+        [wide(narrow(jnp.dot(p[u][j], values[u][j], preferred_element_type=jnp.float32))) for j in both]
+        for u in each
+    ]
+    peak = [jnp.maximum(top[u][0], top[u][1]) for u in each]
+    lift = [[jnp.exp((top[u][j] - peak[u]) * SCALE) for j in both] for u in each]
+    inverse = [1.0 / (total[u][0] * lift[u][0] + total[u][1] * lift[u][1]) for u in each]
+    weight = [[lift[u][j] * inverse[u] for j in both] for u in each]
+    merged = [
+        total[u][0] * weight[u][0] * out[u][0] + total[u][1] * weight[u][1] * out[u][1] for u in each
+    ]
+    delta = [jnp.sum(wide(gs[u]) * merged[u], axis=1, keepdims=True) for u in each]
+    full = [[e[u][j] * weight[u][j] for j in both] for u in each]
+    ds = [
+        [narrow(full[u][j] * ((grad[u][j] - delta[u]) * SCALE)) for j in both] for u in each
+    ]
+    parts = [
+        [wide(narrow(jnp.dot(ds[u][j], keys[u][j], preferred_element_type=jnp.float32))) for j in both]
+        for u in each
+    ]
+    d_query = [parts[u][0] + parts[u][1] for u in each]
+    d_keys = [t_dot(jnp.concatenate(ds[u], axis=1), qs[u]) for u in each]
+    d_values = [
+        t_dot(jnp.concatenate([narrow(full[u][j]) for j in both], axis=1), gs[u]) for u in each
+    ]
     return merged, d_query, d_keys, d_values
+
+
+def wide(value):
+    return value.astype(jnp.float32)
 
 
 def attend_kernel(ids, first, second, q_ref, g_ref, tab, att_ref, dq_ref, con, ck, cv):
     spans = q_ref.shape[0] // SPAN
     reads = 2 * spans
+    group = max(n for n in range(1, 8) if spans % n == 0)
     ck[reads] = jnp.zeros(ck.shape[1:], jnp.float32)
     cv[reads] = jnp.zeros(cv.shape[1:], jnp.float32)
 
-    def one(c, carry):
-        rows = pl.ds(pl.multiple_of(c * SPAN, SPAN), SPAN)
-        q, g = q_ref[rows, :], g_ref[rows, :]
-        picks = [ids[2 * c + j] for j in (0, 1)]
-        spots = [(lax.div(n, 2), lax.rem(n, 2)) for n in picks]
-        keys = [tab[0, o, 0, s] for o, s in spots]
-        values = [tab[0, o, 1, s] for o, s in spots]
-        merged, d_query, d_keys, d_values = span_math(q, g, keys, values)
-        att_ref[rows, :] = merged.astype(jnp.bfloat16)
-        dq_ref[rows, :] = d_query.astype(jnp.bfloat16)
-        for j in (0, 1):
-            ck[2 * c + j] = d_keys[j]
-            cv[2 * c + j] = d_values[j]
+    def some(i, carry):
+        spots = [i * group + u for u in range(group)]
+        rows = [pl.ds(pl.multiple_of(c * SPAN, SPAN), SPAN) for c in spots]
+        qs, gs = [q_ref[r, :] for r in rows], [g_ref[r, :] for r in rows]
+        picks = [[ids[2 * c + j] for j in (0, 1)] for c in spots]
+        keys = [[tab[0, lax.div(n, 2), 0, lax.rem(n, 2)] for n in two] for two in picks]
+        values = [[tab[0, lax.div(n, 2), 1, lax.rem(n, 2)] for n in two] for two in picks]
+        merged, d_query, d_keys, d_values = spans_math(qs, gs, keys, values)
+        for u, c in enumerate(spots):
+            att_ref[rows[u], :] = merged[u].astype(jnp.bfloat16)
+            dq_ref[rows[u], :] = d_query[u].astype(jnp.bfloat16)
+            for j in (0, 1):
+                ck[2 * c + j] = d_keys[u][j * NBR_LEN : (j + 1) * NBR_LEN]
+                cv[2 * c + j] = d_values[u][j * NBR_LEN : (j + 1) * NBR_LEN]
         return carry
 
-    lax.fori_loop(0, spans, one, 0, unroll=2)
+    lax.fori_loop(0, spans // group, some, 0)
 
     def fold(o, carry):
         for s in (0, 1):
@@ -267,10 +286,6 @@
     )(ids, first, second, query_shift, grad_shift, tables)
 
 
-def wide(value):
-    return value.astype(jnp.float32)
-
-
 def scatter_kernel(con, out, acc, sib, r1, r2, r3, r4, send_sem, recv_sem, own_sem):
     y, z, c = place()
     greet(y, z, c)

time: 417 us -> 304 us (0.73)
  Pallas kernels: 364 us -> 251 us
    pallas_call x1, Pallas kernels: 147 us -> 33.8 us  [attend(): pl.pallas_call(attend_kernel, grid_spec=pltpu.PrefetchScalarGridSpec(num_...]
  transfers between devices with their start and end apart: 3 -> 3, of which waited for: 0 -> 0; matrix products, arithmetic and copies ran while one was open for 8% -> 10% of each run, Pallas kernels for 28% -> 39%
where the time goes in v2:
time: 304 us; the launch traced here: 303 us
  Pallas kernels  251 us (83%)
  matrix products  23.1 us (8%)
  local copies, waits for them, and re-layouts  11.2 us (4%)
  other arithmetic  9.16 us (3%)
  starting transfers between devices  7.69 us (3%)
    pallas_call x1, Pallas kernels, scatter_tables(): pl.pallas_call(scatter_kernel, out_shape=jax.ShapeDtypeStruct((heads, 2)...  98.7 us
    pallas_call x1, Pallas kernels, gather_tables(): pl.pallas_call(gather_kernel, out_shape=jax.ShapeDtypeStruct((heads, RING...  97.2 us
    pallas_call x1, Pallas kernels, attend(): pl.pallas_call(attend_kernel, grid_spec=pltpu.PrefetchScalarGridSpec(num_...  33.8 us
    pallas_call x1, Pallas kernels, scatter_enc(): pl.pallas_call(enc_kernel, out_shape=jax.ShapeDtypeStruct((rows, width),...  21.2 us
    dot_general x2, matrix products, per_device(): lax.dot_general(rows, w, contract, preferred_element_type=jnp.float32)  11.7 us
    dot_general x2, matrix products, per_device(): jnp.dot(enc_flat, w, preferred_element_type=jnp.float32)  11.4 us
    ppermute x3, starting transfers between devices, shifted(): lax.ppermute(value, axis, [(source, source + steps) for source in range(f...  7.69 us
  transfers between devices with their start and end apart: 3, of which 0 were waited for; matrix products, arithmetic and copies ran while one was open for 10% of the time, Pallas kernels for 39%

profile of v2, /device:TPU:1, one launch (start us, length us, event | category | flops | bytes accessed | tf_op | source)
XLA Modules:
  0.0 302.9 jit_solution(7189743487936176770)
XLA Ops:
  0.6 1.1 slice_bitcast_fusion.4
  1.8 0.7 pad_maximum_fusion.5
  2.5 3.3 %collective-permute-start = (bf16[2,63,1024]{2,1,0:T(8,128)(2,1)}, bf16[2,63,1024]{2,1,0:T(8,128)(2,1)S(1)}, u32[]{:S(2)}, u32[]{:S(2)}) collective-permute-start(bf16[2,63,1024]{2,1,0:T(8,128)(2,1)} %pad_maximum_fusion.5), channel_id=1, source_target_pairs={{1,0},{2,1},{3,2},{4,3},{5,4},{6,5},{7,6},{8,7},{9,8},{10,9},{11,1... | collective-permute-start | bytes 774152 | tf_op jit(solution)/shard_map/ppermute | solution.py:506
  5.8 0.7 multiply_add_fusion
  6.5 0.1 copy.18
  6.7 5.7 %convolution_convert_fusion = bf16[256,1024]{1,0:T(8,128)(2,1)S(1)} fusion(bf16[256,4096]{1,0:T(8,128)(2,1)S(1)} %bitcast.39, bf16[4096,1024]{1,0:T(8,128)(2,1)} %param.11), kind=kOutput, calls=%fused_computation.5 | convolution fusion | flops 2147745792 | bytes 11010048 | tf_op jit(solution)/shard_map/dot_general | solution.py:530
  12.5 0.2 copy.21
  12.7 0.3 copy.22
  13.0 5.7 %convolution_convert_fusion.1 = bf16[256,1024]{1,0:T(8,128)(2,1)S(1)} fusion(bf16[256,4096]{1,0:T(8,128)(2,1)S(1)} %bitcast.38, bf16[4096,1024]{1,0:T(8,128)(2,1)} %param.10), kind=kOutput, calls=%fused_computation.6 | convolution fusion | flops 2147745792 | bytes 11010048 | tf_op jit(solution)/shard_map/dot_general | solution.py:530
  18.7 0.2 copy.19
  18.9 0.3 copy.20
  19.2 1.1 pad_maximum_fusion.4.own
  20.3 3.2 %slice.36 = bf16[833,1024]{1,0:T(8,128)(2,1)} slice(bf16[896,1024]{1,0:T(8,128)(2,1)} %param.7), slice={[63:896], [0:1024]} | slice | bytes 3411968 | tf_op jit(solution)/shard_map/slice | solution.py:525
  23.5 0.4 slice.40
  24.0 97.2 %gather_tables.1 = bf16[8,4,4,2,2,256,128]{6,5,4,3,2,1,0:T(8,128)(2,1)} custom-call(bf16[8,2,256,128]{3,2,1,0:T(8,128)(2,1)} %pad_maximum_fusion.4.own), custom_call_target="tpu_custom_call" | custom-call | tf_op jit(solution)/shard_map/gather_tables/pallas_call | solution.py:155
  121.3 1.7 pad_maximum_fusion.q_ref
  123.0 1.5 pad_maximum_fusion.1.g_ref
  124.4 33.8 %attend.1 = (bf16[896,1024]{1,0:T(8,128)(2,1)S(1)}, bf16[896,1024]{1,0:T(8,128)(2,1)S(1)}, bf16[8,32,2,2,128,128]{5,4,3,2,1,0:T(8,128)(2,1)}) custom-call(s32[28]{0:T(128)S(1)} %reshape.34.ids, s32[64]{0:T(128)S(1)} %get-tuple-element.10.first, s32[64]{0:T(128)S(1)} %compare_select_fusion.second, bf16[896,1024]{1,0:T(8,128)(2,1)S(1)} %pad_maximum_fusion.q_ref, ...), custom_call_target="tpu_custom_call" | custom-call | tf_op jit(solution)/shard_map/attend/pallas_call | solution.py:267
  158.3 1.3 slice.43
  159.6 1.3 slice.45
  161.0 98.7 %scatter_tables.1 = bf16[8,2,256,128]{3,2,1,0:T(8,128)(2,1)} custom-call(bf16[8,4,4,2,2,256,128]{6,5,4,3,2,1,0:T(8,128)(2,1)} %bitcast.42), custom_call_target="tpu_custom_call" | custom-call | tf_op jit(solution)/shard_map/scatter_tables/pallas_call | solution.py:407
  259.6 1.3 slice_bitcast_fusion
  260.9 0.2 copy.24
  261.2 2.3 collective-permute-start.2
  263.4 2.1 collective-permute-start.1
  265.5 0.2 copy.23
  265.8 5.8 %fusion = f32[256,4096]{1,0:T(8,128)S(1)} fusion(bf16[256,1024]{0,1:T(8,128)(2,1)S(1)} %bitcast.48, bf16[4096,1024]{1,0:T(8,128)(2,1)} %param.10), kind=kOutput, calls=%fused_computation.20 | convolution fusion | flops 2147483648 | bytes 13107200 | tf_op jit(solution)/shard_map/dot_general | solution.py:547
  271.5 5.9 %convolution_add_fusion.part = f32[256,4096]{1,0:T(8,128)S(1)} fusion(f32[256,4096]{1,0:T(8,128)S(1)} %fusion, bf16[256,1024]{0,1:T(8,128)(2,1)S(1)} %bitcast.47, bf16[4096,1024]{1,0:T(8,128)(2,1)} %param.11), kind=kOutput, calls=%fused_computation | convolution fusion | flops 2148532224 | bytes 17301504 | tf_op jit(solution)/shard_map/dot_general | solution.py:547
  277.4 21.2 %scatter_enc.1 = bf16[256,1024]{1,0:T(8,128)(2,1)S(1)} custom-call(f32[256,4096]{1,0:T(8,128)S(1)} %convolution_add_fusion.part), custom_call_target="tpu_custom_call" | custom-call | tf_op jit(solution)/shard_map/scatter_enc/pallas_call | solution.py:483
  298.7 1.7 pad_maximum_fusion.3
  300.4 1.7 pad_maximum_fusion.2
  302.1 0.8 copy.26
  (19 shorter events, 0.3 us)
Async XLA Ops:
  0.6 6.1 %copy-start = (bf16[2,128,4096]{2,1,0:T(8,128)(2,1)S(1)}, bf16[2,128,4096]{2,1,0:T(8,128)(2,1)}, u32[]{:S(2)}) copy-start(bf16[2,128,4096]{2,1,0:T(8,128)(2,1)} %param.9) | copy-start | bytes 6291460
  2.5 118.7 %collective-permute-start = (bf16[2,63,1024]{2,1,0:T(8,128)(2,1)}, bf16[2,63,1024]{2,1,0:T(8,128)(2,1)S(1)}, u32[]{:S(2)}, u32[]{:S(2)}) collective-permute-start(bf16[2,63,1024]{2,1,0:T(8,128)(2,1)} %pad_maximum_fusion.5), channel_id=1, source_target_pairs={{1,0},{2,1},{3,2},{4,3},{5,4},{6,5},{7,6},{8,7},{9,8},{10,9},{11,1... | collective-permute-start | bytes 774152 | tf_op jit(solution)/shard_map/ppermute | solution.py:506
  20.2 3.3 %copy-start.4 = (bf16[896,1024]{1,0:T(8,128)(2,1)S(1)}, bf16[896,1024]{1,0:T(8,128)(2,1)}, u32[]{:S(2)}) copy-start(bf16[896,1024]{1,0:T(8,128)(2,1)} %param.8) | copy-start | bytes 5505028
  261.2 37.5 %collective-permute-start.2 = (bf16[63,1024]{1,0:T(8,128)(2,1)S(1)}, bf16[63,1024]{1,0:T(8,128)(2,1)S(1)}, u32[]{:S(2)}, u32[]{:S(2)}) collective-permute-start(bf16[63,1024]{1,0:T(8,128)(2,1)S(1)} %slice.44), channel_id=1, source_target_pairs={{0,1},{1,2},{2,3},{3,4},{4,5},{5,6},{6,7},{7,8},{8,9},{9,10},{10,1... | collective-permute-start | bytes 387080 | tf_op jit(solution)/shard_map/ppermute | solution.py:506
  263.4 37.0 %collective-permute-start.1 = (bf16[63,1024]{1,0:T(8,128)(2,1)S(1)}, bf16[63,1024]{1,0:T(8,128)(2,1)S(1)}, u32[]{:S(2)}, u32[]{:S(2)}) collective-permute-start(bf16[63,1024]{1,0:T(8,128)(2,1)S(1)} %slice.42), channel_id=1, source_target_pairs={{0,1},{1,2},{2,3},{3,4},{4,5},{5,6},{6,7},{7,8},{8,9},{9,10},{10,1... | collective-permute-start | bytes 387080 | tf_op jit(solution)/shard_map/ppermute | solution.py:506
  277.4 21.2 %copy-start.3 = (bf16[833,1024]{1,0:T(8,128)(2,1)S(1)}, bf16[833,1024]{1,0:T(8,128)(2,1)}, u32[]{:S(2)}) copy-start(bf16[833,1024]{1,0:T(8,128)(2,1)} %slice.45) | copy-start | bytes 5117956
  298.7 1.7 copy-start.2
  298.7 4.2 %copy-start.1 = (bf16[2,128,4096]{2,1,0:T(8,128)(2,1)S(1)}, bf16[2,128,4096]{2,1,0:T(8,128)(2,1)}, u32[]{:S(2)}) copy-start(bf16[2,128,4096]{2,1,0:T(8,128)(2,1)} %param.9) | copy-start | bytes 6291460

commit v3 on v2

v3 whole, which is shorter than its diff:
```python
import math

import jax
import jax.numpy as jnp
from jax import lax
from jax.experimental import pallas as pl
from jax.experimental.pallas import tpu as pltpu
from jax.sharding import PartitionSpec as P

HD = 128
SPAN = 64
NBR_LEN = 128
MESH = pl.DeviceIdType.MESH
SCALE = 1.0 / math.sqrt(HD)
RING = 4
MIB = 1024 * 1024


def place():
    s = lax.axis_index("seq")
    return lax.div(s, 8), lax.rem(lax.div(s, 2), RING), lax.rem(s, 2)


def up(i):
    return lax.rem(i + 1, RING)


def down(i):
    return lax.rem(i + RING - 1, RING)


def across(i):
    return lax.rem(i + 2, RING)


def index_of(y, z, c):
    return y * 8 + z * 2 + c


def greet(y, z, c):
    barrier = pltpu.get_barrier_semaphore()
    for other in (
        index_of(up(y), z, c),
        index_of(down(y), z, c),
        index_of(y, up(z), c),
        index_of(y, down(z), c),
        index_of(y, z, 1 - c),
    ):
        pl.semaphore_signal(barrier, inc=1, device_id={"seq": other}, device_id_type=MESH)
    pl.semaphore_wait(barrier, 5)


def dot_t(a, b):
    return lax.dot_general(a, b, (((1,), (1,)), ((), ())), preferred_element_type=jnp.float32)


def t_dot(a, b):
    return lax.dot_general(a, b, (((0,), (0,)), ((), ())), preferred_element_type=jnp.float32)


def spans_math(qs, gs, keys, values):
    each, both = range(len(qs)), (0, 1)

    def pairs(rows, tables):
        joined = [dot_t(rows[u], jnp.concatenate(tables[u], axis=0)) for u in each]
        return [[x[:, :NBR_LEN], x[:, NBR_LEN:]] for x in joined]

    def narrow(x):
        return x.astype(jnp.bfloat16)

    s = pairs(qs, keys)
    grad = pairs(gs, values)
    top = [[jnp.max(s[u][j], axis=1, keepdims=True) for j in both] for u in each]
    e = [[jnp.exp((s[u][j] - top[u][j]) * SCALE) for j in both] for u in each]
    total = [[jnp.sum(e[u][j], axis=1, keepdims=True) for j in both] for u in each]
    p = [[narrow(e[u][j] * (1.0 / total[u][j])) for j in both] for u in each]
    out = [
        [wide(narrow(jnp.dot(p[u][j], values[u][j], preferred_element_type=jnp.float32))) for j in both]
        for u in each
    ]
    peak = [jnp.maximum(top[u][0], top[u][1]) for u in each]
    lift = [[jnp.exp((top[u][j] - peak[u]) * SCALE) for j in both] for u in each]
    inverse = [1.0 / (total[u][0] * lift[u][0] + total[u][1] * lift[u][1]) for u in each]
    weight = [[lift[u][j] * inverse[u] for j in both] for u in each]
    merged = [
        total[u][0] * weight[u][0] * out[u][0] + total[u][1] * weight[u][1] * out[u][1] for u in each
    ]
    delta = [jnp.sum(wide(gs[u]) * merged[u], axis=1, keepdims=True) for u in each]
    full = [[e[u][j] * weight[u][j] for j in both] for u in each]
    ds = [
        [narrow(full[u][j] * ((grad[u][j] - delta[u]) * SCALE)) for j in both] for u in each
    ]
    parts = [
        [wide(narrow(jnp.dot(ds[u][j], keys[u][j], preferred_element_type=jnp.float32))) for j in both]
        for u in each
    ]
    d_query = [parts[u][0] + parts[u][1] for u in each]
    d_keys = [t_dot(jnp.concatenate(ds[u], axis=1), qs[u]) for u in each]
    d_values = [
        t_dot(jnp.concatenate([narrow(full[u][j]) for j in both], axis=1), gs[u]) for u in each
    ]
    return merged, d_query, d_keys, d_values


def wide(value):
    return value.astype(jnp.float32)


def core_kernel(
    ids, first, second, own, q_ref, g_ref,
    att_ref, dq_ref, out, tab, landed,
    table_even, table_odd, ck, cv, acc, give_even, give_odd, got_even, got_odd,
    r1, r2, r3, r4, send_sem, recv_sem, back_send, back_recv, own_sem, load_sem,
):
    y, z, c = place()
    greet(y, z, c)
    pairs = own.shape[0] // 2
    spans = q_ref.shape[0] // SPAN
    reads = 2 * spans
    group = max(n for n in range(1, 8) if spans % n == 0)
    sibling = index_of(y, z, 1 - c)
    every = slice(None)
    held = (table_even, table_odd)
    give = (give_even, give_odd)
    got = (got_even, got_odd)
    ck[reads] = jnp.zeros(ck.shape[1:], jnp.float32)
    cv[reads] = jnp.zeros(cv.shape[1:], jnp.float32)

    class Head:
        def __init__(self, h, parity):
            self.h, self.parity = h, parity
            self.f, self.g = (y, z) if parity == 0 else (z, y)

        def dev(self, a, b):
            return index_of(a, b, c) if self.parity == 0 else index_of(b, a, c)

        def spot(self, a, b):
            return (self.h, a, b) if self.parity == 0 else (self.h, b, a)

        def block(self, a, *half):
            return tab.at[self.spot(a, self.g) + (c,) + half]

        def band(self, b, *half):
            return tab.at[self.spot(every, b) + (c,) + half]

        def mine(self):
            return pltpu.make_async_copy(own.at[self.h], self.block(self.f), own_sem.at[self.h])

        def load(self):
            return pltpu.make_async_copy(
                tab.at[self.h], held[self.parity], load_sem.at[self.h, 0]
            )

        def fetch(self):
            return pltpu.make_async_copy(
                landed.at[self.h], got[self.parity], load_sem.at[self.h, 1]
            )

        def out_move(self, kind):
            f, g, dev = self.f, self.g, self.dev
            if kind < 4:
                src = (own.at[self.h], own.at[self.h], None, None)[kind]
                dst = (
                    lambda: self.block(f),
                    lambda: self.block(f),
                    lambda: self.block(down(f), 0),
                    lambda: self.block(up(f), 1),
                )[kind]()
                to = dev(up(f), g) if kind % 2 == 0 else dev(down(f), g)
            elif kind < 8:
                dst = (
                    lambda: self.band(g),
                    lambda: self.band(g),
                    lambda: self.band(down(g), slice(0, 1)),
                    lambda: self.band(up(g), slice(1, 2)),
                )[kind - 4]()
                src, to = None, dev(f, up(g)) if kind % 2 == 0 else dev(f, down(g))
            else:
                dst = self.band((g, down(g), up(g), across(g))[kind - 8])
                src, to = None, sibling
            return pltpu.make_async_remote_copy(
                src_ref=dst if src is None else src,
                dst_ref=dst,
                send_sem=send_sem.at[self.h, kind],
                recv_sem=recv_sem.at[self.h, kind],
                device_id={"seq": to},
                device_id_type=MESH,
            )

        def back_move(self, kind):
            f, g, dev, h = self.f, self.g, self.dev, self.h
            src, dst, to = (
                lambda: (give[self.parity], landed.at[h], sibling),
                lambda: (acc.at[self.spot(every, across(g)) + (0,)], r1.at[h, 0], dev(f, up(g))),
                lambda: (acc.at[self.spot(every, across(g)) + (1,)], r1.at[h, 1], dev(f, down(g))),
                lambda: (acc.at[self.spot(every, up(g))], r2.at[h, 0], dev(f, up(g))),
                lambda: (acc.at[self.spot(every, down(g))], r2.at[h, 1], dev(f, down(g))),
                lambda: (acc.at[self.spot(across(f), g) + (0,)], r3.at[h, 0], dev(up(f), g)),
                lambda: (acc.at[self.spot(across(f), g) + (1,)], r3.at[h, 1], dev(down(f), g)),
                lambda: (acc.at[self.spot(up(f), g)], r4.at[h, 0], dev(up(f), g)),
                lambda: (acc.at[self.spot(down(f), g)], r4.at[h, 1], dev(down(f), g)),
            )[kind]()
            return pltpu.make_async_remote_copy(
                src_ref=src,
                dst_ref=dst,
                send_sem=back_send.at[h, kind],
                recv_sem=back_recv.at[h, kind],
                device_id={"seq": to},
                device_id_type=MESH,
            )

    def own_out(t):
        t.mine().start()
        t.out_move(0).start()
        t.out_move(1).start()

    def block_on(t):
        t.out_move(0).wait_recv()
        t.out_move(2).start()
        t.out_move(1).wait_recv()
        t.out_move(3).start()

    def band_out(t):
        t.mine().wait()
        t.out_move(2).wait_recv()
        t.out_move(3).wait_recv()
        t.out_move(4).start()
        t.out_move(5).start()
        t.out_move(8).start()

    def band_on(t):
        t.out_move(4).wait_recv()
        t.out_move(6).start()
        t.out_move(9).start()
        t.out_move(5).wait_recv()
        t.out_move(7).start()
        t.out_move(10).start()

    def band_last(t):
        t.out_move(6).wait_recv()
        t.out_move(7).wait_recv()
        t.out_move(11).start()

    def table_in(t):
        for kind in (8, 9, 10, 11):
            t.out_move(kind).wait_recv()
        t.load().start()
        for kind in range(12):
            t.out_move(kind).wait_send()

    def sibling_in(t):
        t.back_move(0).wait_recv()
        t.fetch().start()
        t.back_move(0).wait_send()

    def attend(t):
        table, cols = held[t.parity], pl.ds(pl.multiple_of(t.h * HD, HD), HD)
        t.load().wait()

        def pick(n, kv):
            return table[lax.div(n, 16), lax.rem(lax.div(n, 4), RING), lax.rem(lax.div(n, 2), 2), kv, lax.rem(n, 2)]

        def some(i, carry):
            spots = [i * group + u for u in range(group)]
            rows = [pl.ds(pl.multiple_of(s * SPAN, SPAN), SPAN) for s in spots]
            qs, gs = [q_ref[r, cols] for r in rows], [g_ref[r, cols] for r in rows]
            picks = [[ids[2 * s + j] for j in (0, 1)] for s in spots]
            keys = [[pick(n, 0) for n in two] for two in picks]
            values = [[pick(n, 1) for n in two] for two in picks]
            merged, d_query, d_keys, d_values = spans_math(qs, gs, keys, values)
            for u, s in enumerate(spots):
                att_ref[rows[u], cols] = merged[u].astype(jnp.bfloat16)
                dq_ref[rows[u], cols] = d_query[u].astype(jnp.bfloat16)
                for j in (0, 1):
                    ck[2 * s + j] = d_keys[u][j * NBR_LEN : (j + 1) * NBR_LEN]
                    cv[2 * s + j] = d_values[u][j * NBR_LEN : (j + 1) * NBR_LEN]
            return carry

        lax.fori_loop(0, spans // group, some, 0)

        def fold(chip, carry):
            a, b = lax.div(chip, RING), lax.rem(chip, RING)
            for s in (0, 1):
                for core, keep in ((c, True), (1 - c, False)):
                    n = (2 * chip + core) * 2 + s
                    one, two = first[n], second[n]
                    for kv, part in ((0, ck), (1, cv)):
                        total = (part[one] + part[two]).astype(jnp.bfloat16)
                        lines = pl.ds(s * NBR_LEN, NBR_LEN)
                        if keep:
                            acc[t.h, a, b, kv, lines] = total
                        else:
                            give[t.parity][a, b, kv, lines] = total
            return carry

        lax.fori_loop(0, RING * RING, fold, 0)
        t.back_move(0).start()

    def sum_sibling(t):
        t.fetch().wait()

        def add(i, carry):
            a, b = lax.div(i, RING), lax.rem(i, RING)
            for kv in (0, 1):
                acc[t.h, a, b, kv] = acc[t.h, a, b, kv] + got[t.parity][a, b, kv]
            return carry

        lax.fori_loop(0, RING * RING, add, 0)
        t.back_move(1).start()
        t.back_move(2).start()

    def sum_band_half(t):
        for half, (kind, toward) in enumerate(((1, up(t.g)), (2, down(t.g)))):
            t.back_move(kind).wait_recv()

            def add(a, carry):
                at = t.spot(a, toward) + (half,)
                acc[at] = acc[at] + r1[t.h, half, a]
                return carry

            lax.fori_loop(0, RING, add, 0)
            t.back_move(3 + half).start()

    def sum_band(t):
        t.back_move(3).wait_recv()
        t.back_move(4).wait_recv()

        def add(a, carry):
            for kv in (0, 1):
                at = t.spot(a, t.g) + (kv,)
                total = wide(acc[at]) + wide(r2[t.h, 0, a, kv]) + wide(r2[t.h, 1, a, kv])
                acc[at] = total.astype(jnp.bfloat16)
            return carry

        lax.fori_loop(0, RING, add, 0)
        t.back_move(5).start()
        t.back_move(6).start()

    def sum_block_half(t):
        for half, (kind, toward) in enumerate(((5, up(t.f)), (6, down(t.f)))):
            t.back_move(kind).wait_recv()
            at = t.spot(toward, t.g) + (half,)
            acc[at] = acc[at] + r3[t.h, half]
            t.back_move(7 + half).start()

    def sum_block(t):
        t.back_move(7).wait_recv()
        t.back_move(8).wait_recv()
        for kv in (0, 1):
            total = wide(acc[t.spot(t.f, t.g) + (kv,)])
            total = total + wide(r4[t.h, 0, kv]) + wide(r4[t.h, 1, kv])
            out[t.h, kv] = total.astype(jnp.bfloat16)
        for kind in range(1, 9):
            t.back_move(kind).wait_send()

    stages = (
        (0, own_out),
        (1, block_on),
        (2, band_out),
        (3, band_on),
        (4, band_last),
        (5, table_in),
        (6, sibling_in),
        (10, sum_block),
        (9, sum_block_half),
        (8, sum_band),
        (7, sum_band_half),
        (5, attend),
        (6, sum_sibling),
    )

    def step(i, carry):
        for lag, stage in stages:

            @pl.when((i >= lag) & (i < pairs + lag))
            def _(lag=lag, stage=stage):
                for parity in (0, 1):
                    stage(Head(2 * (i - lag) + parity, parity))

        return carry

    lax.fori_loop(0, pairs + max(lag for lag, _ in stages), step, 0)


def core(ids, first, second, own, query_shift, grad_shift):
    rows, width = query_shift.shape
    heads, reads = own.shape[0], ids.shape[0]
    rest = own.shape[1:]
    tail = (2, 2 * NBR_LEN, HD)
    bf16, f32 = jnp.bfloat16, jnp.float32
    in_vmem = pl.BlockSpec(memory_space=pltpu.VMEM)
    in_smem = pl.BlockSpec(memory_space=pltpu.SMEM)
    anywhere = pl.BlockSpec(memory_space=pl.ANY)
    band = (RING, RING) + tail
    dma = pltpu.SemaphoreType.DMA
    return pl.pallas_call(
        core_kernel,
        in_specs=[in_smem, in_smem, in_smem, anywhere, in_vmem, in_vmem],
        out_specs=[in_vmem, in_vmem, in_vmem, anywhere, anywhere],
        out_shape=[
            jax.ShapeDtypeStruct((rows, width), bf16),
            jax.ShapeDtypeStruct((rows, width), bf16),
            jax.ShapeDtypeStruct((heads,) + tail, bf16),
            jax.ShapeDtypeStruct((heads, RING, RING, 2) + rest, bf16),
            jax.ShapeDtypeStruct((heads,) + band, bf16),
        ],
        scratch_shapes=[
            pltpu.VMEM((RING, RING, 2) + rest, bf16),
            pltpu.VMEM((RING, RING, 2) + rest, bf16),
            pltpu.VMEM((reads + 1, NBR_LEN, HD), f32),
            pltpu.VMEM((reads + 1, NBR_LEN, HD), f32),
            pltpu.VMEM((heads,) + band, bf16),
            pltpu.VMEM(band, bf16),
            pltpu.VMEM(band, bf16),
            pltpu.VMEM(band, bf16),
            pltpu.VMEM(band, bf16),
            pltpu.VMEM((heads, 2, RING) + tail[1:], bf16),
            pltpu.VMEM((heads, 2, RING) + tail, bf16),
            pltpu.VMEM((heads, 2) + tail[1:], bf16),
            pltpu.VMEM((heads, 2) + tail, bf16),
            dma((heads, 12)),
            dma((heads, 12)),
            dma((heads, 9)),
            dma((heads, 9)),
            dma((heads,)),
            dma((heads, 2)),
        ],
        compiler_params=pltpu.CompilerParams(
            collective_id=0, has_side_effects=True, vmem_limit_bytes=63 * MIB
        ),
        name="core",
    )(ids, first, second, own, query_shift, grad_shift)


def enc_kernel(part, out, s1, s2, r1, r2, send_sem, recv_sem):
    x = lax.axis_index("enc")
    right, left = up(x), down(x)
    barrier = pltpu.get_barrier_semaphore()
    for other in (right, left):
        pl.semaphore_signal(barrier, inc=1, device_id={"enc": other}, device_id_type=MESH)
    pl.semaphore_wait(barrier, 2)
    rows = part.shape[0]
    half = rows // 2
    width = out.shape[1]

    def cols(t):
        return pl.ds(pl.multiple_of(t * width, width), width)

    def remote(kind, src, dst, to):
        return pltpu.make_async_remote_copy(
            src_ref=src,
            dst_ref=dst,
            send_sem=send_sem.at[kind],
            recv_sem=recv_sem.at[kind],
            device_id={"enc": to},
            device_id_type=MESH,
        )

    moves = [
        remote(0, s1.at[0], r1.at[0], right),
        remote(1, s1.at[1], r1.at[1], left),
        remote(2, s2.at[0], r2.at[0], right),
        remote(3, s2.at[1], r2.at[1], left),
    ]
    far = cols(across(x))
    s1[0] = part[:half, far].astype(jnp.bfloat16)
    moves[0].start()
    s1[1] = part[half:, far].astype(jnp.bfloat16)
    moves[1].start()
    s2[0, half:] = part[half:, cols(right)].astype(jnp.bfloat16)
    s2[1, :half] = part[:half, cols(left)].astype(jnp.bfloat16)
    moves[0].wait_recv()
    s2[0, :half] = (part[:half, cols(right)] + wide(r1[0])).astype(jnp.bfloat16)
    moves[2].start()
    moves[1].wait_recv()
    s2[1, half:] = (part[half:, cols(left)] + wide(r1[1])).astype(jnp.bfloat16)
    moves[3].start()
    moves[2].wait_recv()
    moves[3].wait_recv()
    out[...] = (part[:, cols(x)] + wide(r2[0]) + wide(r2[1])).astype(jnp.bfloat16)
    for move in moves:
        move.wait_send()


def scatter_enc(part):
    rows, width = part.shape[0], part.shape[1] // RING
    half = rows // 2
    return pl.pallas_call(
        enc_kernel,
        out_shape=jax.ShapeDtypeStruct((rows, width), jnp.bfloat16),
        in_specs=[pl.BlockSpec(memory_space=pltpu.VMEM)],
        out_specs=pl.BlockSpec(memory_space=pltpu.VMEM),
        scratch_shapes=[
            pltpu.VMEM((2, half, width), jnp.bfloat16),
            pltpu.VMEM((2, rows, width), jnp.bfloat16),
            pltpu.VMEM((2, half, width), jnp.bfloat16),
            pltpu.VMEM((2, rows, width), jnp.bfloat16),
            pltpu.SemaphoreType.DMA((4,)),
            pltpu.SemaphoreType.DMA((4,)),
        ],
        compiler_params=pltpu.CompilerParams(
            collective_id=2, has_side_effects=True, vmem_limit_bytes=32 * MIB
        ),
        name="scatter_enc",
    )(part)


def shifted(value, axis, steps):
    count = lax.axis_size(axis)
    first, last = (max(0, -steps), min(count, count - steps))
    return lax.ppermute(value, axis, [(source, source + steps) for source in range(first, last)])


def per_device(queries, d_attended, encodings, w_key, w_value, neighbour_owner, neighbour_slot):
    tok_rows, feat_width = queries.shape
    heads = feat_width // HD
    margin = SPAN - 1
    owned = encodings.shape[0]
    owners = lax.axis_size("seq")
    reads = 2 * (tok_rows // SPAN)

    ids = (neighbour_owner * owned + neighbour_slot).reshape(reads).astype(jnp.int32)
    hit = ids[None, :] == jnp.arange(owners * owned, dtype=jnp.int32)[:, None]
    order = jnp.arange(reads, dtype=jnp.int32)[None, :]
    first = jnp.min(jnp.where(hit, order, reads), axis=1)
    last = jnp.max(jnp.where(hit, order, -1), axis=1)
    second = jnp.where(last > first, last, reads)

    rim_rows = shifted(jnp.stack([queries[:margin], d_attended[:margin]]), "seq", -1)
    query_shift = jnp.concatenate([queries[margin:], rim_rows[0]], axis=0)
    grad_shift = jnp.concatenate([d_attended[margin:], rim_rows[1]], axis=0)

    enc_flat = encodings.reshape(owned * NBR_LEN, encodings.shape[2])
    tables = [
        jnp.dot(enc_flat, w, preferred_element_type=jnp.float32)
        .astype(jnp.bfloat16)
        .reshape(owned, NBR_LEN, heads, HD)
        .transpose(2, 0, 1, 3)
        for w in (w_key, w_value)
    ]
    attended_shift, dq_shift, grads, _, _ = core(
        ids, first, second, jnp.stack(tables, axis=1), query_shift, grad_shift
    )
    attended_tail = shifted(attended_shift[tok_rows - margin :], "seq", 1)
    query_tail = shifted(dq_shift[tok_rows - margin :], "seq", 1)
    contract = (((1,), (1,)), ((), ()))
    part = 0.0
    for kv, w in enumerate((w_key, w_value)):
        rows = grads[:, kv].transpose(1, 0, 2).reshape(owned * NBR_LEN, feat_width)
        part = part + lax.dot_general(rows, w, contract, preferred_element_type=jnp.float32)
    d_encodings = scatter_enc(part).reshape(owned, NBR_LEN, feat_width)
    attended = jnp.concatenate([attended_tail, attended_shift[: tok_rows - margin]], axis=0)
    d_queries = jnp.concatenate([query_tail, dq_shift[: tok_rows - margin]], axis=0)
    return (attended, d_queries, d_encodings)


def solution(mesh):
    return jax.shard_map(
        per_device,
        mesh=mesh,
        in_specs=(
            P("seq", "enc"),
            P("seq", "enc"),
            P("seq", None, None),
            P(None, "enc"),
            P(None, "enc"),
            P("seq", None),
            P("seq", None),
        ),
        out_specs=(P("seq", "enc"), P("seq", "enc"), P("seq", None, "enc")),
        check_vma=False,
    )
```

time: 304 us -> 273 us (0.90)
  Pallas kernels: 251 us -> 209 us
  starting transfers between devices: 7.69 us -> 13.1 us
    pallas_call x3 -> x1, Pallas kernels: 230 us -> 189 us  [core(): pl.pallas_call(core_kernel, in_specs=[in_smem, in_smem, in_smem, anywhere...]
    ppermute x3, starting transfers between devices: 7.69 us -> 13.1 us  [shifted(): lax.ppermute(value, axis, [(source, source + steps) for source in range(f...]
    transpose x3, local copies, waits for them, and re-layouts: 1.73 us -> 5.13 us  [per_device(): rows = grads[:, kv].transpose(1, 0, 2).reshape(owned * NBR_LEN, feat_width)]
  transfers between devices with their start and end apart: 3 -> 3, of which waited for: 0 -> 0; matrix products, arithmetic and copies ran while one was open for 10% -> 12% of each run, Pallas kernels for 39% -> 7%
where the time goes in v3:
time: 273 us; the launch traced here: 272 us
  Pallas kernels  209 us (77%)
  matrix products  24.1 us (9%)
  local copies, waits for them, and re-layouts  14.1 us (5%)
  starting transfers between devices  13.1 us (5%)
  other arithmetic  10.6 us (4%)
    pallas_call x1, Pallas kernels, core(): pl.pallas_call(core_kernel, in_specs=[in_smem, in_smem, in_smem, anywhere...  189 us
    pallas_call x1, Pallas kernels, scatter_enc(): pl.pallas_call(enc_kernel, out_shape=jax.ShapeDtypeStruct((rows, width),...  20.2 us
    ppermute x3, starting transfers between devices, shifted(): lax.ppermute(value, axis, [(source, source + steps) for source in range(f...  13.1 us
    dot_general x2, matrix products, per_device(): jnp.dot(enc_flat, w, preferred_element_type=jnp.float32)  12.3 us
    dot_general x2, matrix products, per_device(): lax.dot_general(rows, w, contract, preferred_element_type=jnp.float32)  11.9 us
  transfers between devices with their start and end apart: 3, of which 0 were waited for; matrix products, arithmetic and copies ran while one was open for 12% of the time, Pallas kernels for 7%

profile of v3, /device:TPU:1, one launch (start us, length us, event | category | flops | bytes accessed | tf_op | source)
XLA Modules:
  0.0 271.8 jit_solution(14134007279817188562)
XLA Ops:
  0.6 1.0 slice_bitcast_fusion.4
  1.7 3.3 %collective-permute-start = (bf16[2,63,1024]{2,1,0:T(8,128)(2,1)S(1)}, bf16[2,63,1024]{2,1,0:T(8,128)(2,1)S(1)}, u32[]{:S(2)}, u32[]{:S(2)}) collective-permute-start(bf16[2,63,1024]{2,1,0:T(8,128)(2,1)S(1)} %pad_maximum_fusion.5), channel_id=1, source_target_pairs={{1,0},{2,1},{3,2},{4,3},{5,4},{6,5},{7,6},{8,7},{9,8},{10,9},{11,1... | collective-permute-start | bytes 774152 | tf_op jit(solution)/shard_map/ppermute | solution.py:511
  5.0 0.7 multiply_add_fusion
  5.7 0.1 copy.16
  5.9 6.5 %fusion.1 = bf16[32,8,8,128]{3,1,2,0:T(8,128)(2,1)S(1)} fusion(bf16[256,4096]{1,0:T(8,128)(2,1)} %bitcast.49, bf16[4096,1024]{1,0:T(8,128)(2,1)} %param.11), kind=kOutput, calls=%fused_computation.8 | convolution fusion | flops 2147745792 | bytes 11010048 | tf_op jit(solution)/shard_map/dot_general | solution.py:535
  12.5 5.8 %fusion = bf16[32,8,8,128]{3,1,2,0:T(8,128)(2,1)S(1)} fusion(bf16[256,4096]{1,0:T(8,128)(2,1)S(1)} %bitcast.50, bf16[4096,1024]{1,0:T(8,128)(2,1)} %param.10), kind=kOutput, calls=%fused_computation.7 | convolution fusion | flops 2147745792 | bytes 11010048 | tf_op jit(solution)/shard_map/dot_general | solution.py:535
  18.4 0.2 copy_bitcast_fusion
  18.6 1.1 pad_maximum_fusion.4.own
  19.8 0.5 copy-done
  20.3 0.4 slice.36
  20.7 0.6 copy-done.1
  21.4 0.4 slice.40
  21.8 0.6 compare_select_fusion.second
  22.4 1.5 pad_maximum_fusion.q_ref
  23.9 1.5 pad_maximum_fusion.1.g_ref
  25.3 188.8 %core.1 = (bf16[896,1024]{1,0:T(8,128)(2,1)}, bf16[896,1024]{1,0:T(8,128)(2,1)}, bf16[8,2,256,128]{3,2,1,0:T(8,128)(2,1)}, bf16[8,4,4,2,2,2,128,128]{7,6,5,4,3,2...) custom-call(s32[28]{0:T(128)} %copy-done.5, s32[64]{0:T(128)} %copy-done.6, s32[64]{0:T(128)} %compare_select_fusion.second, ...), custom_call_target="tpu_custom_call" | custom-call | tf_op jit(solution)/shard_map/core/pallas_call | solution.py:396
  214.2 1.7 slice.42
  215.9 1.6 slice.43
  217.5 0.7 slice.44
  218.2 0.1 slice.45
  218.3 0.4 copy-done.3
  218.8 1.0 slice_bitcast_fusion
  219.8 2.0 copy.20
  221.8 7.6 %collective-permute-start.2 = (bf16[63,1024]{1,0:T(8,128)(2,1)}, bf16[63,1024]{1,0:T(8,128)(2,1)}, u32[]{:S(2)}, u32[]{:S(2)}) collective-permute-start(bf16[63,1024]{1,0:T(8,128)(2,1)} %slice.44), channel_id=1, source_target_pairs={{0,1},{1,2},{2,3},{3,4},{4,5},{5,6},{6,7},{7,8},{8,9},{9,10},{10,1... | collective-permute-start | bytes 387080 | tf_op jit(solution)/shard_map/ppermute | solution.py:511
  229.5 2.1 collective-permute-start.1
  231.6 2.0 copy.19
  233.6 6.0 %fusion.2 = f32[256,4096]{1,0:T(8,128)S(1)} fusion(bf16[256,1024]{0,1:T(8,128)(2,1)} %bitcast.48, bf16[4096,1024]{1,0:T(8,128)(2,1)} %param.10), kind=kOutput, calls=%fused_computation.24 | convolution fusion | flops 2147483648 | bytes 13107200 | tf_op jit(solution)/shard_map/dot_general | solution.py:550
  239.7 5.9 %convolution_add_fusion.part = f32[256,4096]{1,0:T(8,128)S(1)} fusion(f32[256,4096]{1,0:T(8,128)S(1)} %fusion.2, bf16[256,1024]{0,1:T(8,128)(2,1)S(1)} %bitcast.47, bf16[4096,1024]{1,0:T(8,128)(2,1)} %param.11), kind=kOutput, calls=%fused_computation | convolution fusion | flops 2148532224 | bytes 17301504 | tf_op jit(solution)/shard_map/dot_general | solution.py:550
  245.6 20.2 %scatter_enc.1 = bf16[256,1024]{1,0:T(8,128)(2,1)S(1)} custom-call(f32[256,4096]{1,0:T(8,128)S(1)} %convolution_add_fusion.part), custom_call_target="tpu_custom_call" | custom-call | tf_op jit(solution)/shard_map/scatter_enc/pallas_call | solution.py:488
  265.8 2.6 pad_maximum_fusion.3
  268.4 2.6 pad_maximum_fusion.2
  271.0 0.8 copy.26
  (22 shorter events, 0.4 us)
Async XLA Ops:
  1.7 20.7 %collective-permute-start = (bf16[2,63,1024]{2,1,0:T(8,128)(2,1)S(1)}, bf16[2,63,1024]{2,1,0:T(8,128)(2,1)S(1)}, u32[]{:S(2)}, u32[]{:S(2)}) collective-permute-start(bf16[2,63,1024]{2,1,0:T(8,128)(2,1)S(1)} %pad_maximum_fusion.5), channel_id=1, source_target_pairs={{1,0},{2,1},{3,2},{4,3},{5,4},{6,5},{7,6},{8,7},{9,8},{10,9},{11,1... | collective-permute-start | bytes 774152 | tf_op jit(solution)/shard_map/ppermute | solution.py:511
  5.9 13.8 %copy-start.5 = (s32[28]{0:T(128)}, s32[28]{0:T(128)S(1)}, u32[]{:S(2)}) copy-start(s32[28]{0:T(128)S(1)} %reshape.28.ids) | copy-start | bytes 340
  5.9 6.6 %copy-start.7 = (bf16[2,128,4096]{2,1,0:T(8,128)(2,1)S(1)}, bf16[2,128,4096]{2,1,0:T(8,128)(2,1)}, u32[]{:S(2)}) copy-start(bf16[2,128,4096]{2,1,0:T(8,128)(2,1)} %param.9) | copy-start | bytes 6291460
  18.4 1.9 copy-start
  19.7 1.6 copy-start.1
  20.3 1.5 copy-start.6
  214.2 3.3 %copy-start.2 = (bf16[896,1024]{1,0:T(8,128)(2,1)S(1)}, bf16[896,1024]{1,0:T(8,128)(2,1)}, u32[]{:S(2)}) copy-start(bf16[896,1024]{1,0:T(8,128)(2,1)} %get-tuple-element.7) | copy-start | bytes 5505028
  217.5 1.3 copy-start.3
  221.8 43.9 %collective-permute-start.2 = (bf16[63,1024]{1,0:T(8,128)(2,1)}, bf16[63,1024]{1,0:T(8,128)(2,1)}, u32[]{:S(2)}, u32[]{:S(2)}) collective-permute-start(bf16[63,1024]{1,0:T(8,128)(2,1)} %slice.44), channel_id=1, source_target_pairs={{0,1},{1,2},{2,3},{3,4},{4,5},{5,6},{6,7},{7,8},{8,9},{9,10},{10,1... | collective-permute-start | bytes 387080 | tf_op jit(solution)/shard_map/ppermute | solution.py:511
  229.5 38.9 %collective-permute-start.1 = (bf16[63,1024]{1,0:T(8,128)(2,1)}, bf16[63,1024]{1,0:T(8,128)(2,1)}, u32[]{:S(2)}, u32[]{:S(2)}) collective-permute-start(bf16[63,1024]{1,0:T(8,128)(2,1)} %slice.42), channel_id=1, source_target_pairs={{0,1},{1,2},{2,3},{3,4},{4,5},{5,6},{6,7},{7,8},{8,9},{9,10},{10,1... | collective-permute-start | bytes 387080 | tf_op jit(solution)/shard_map/ppermute | solution.py:511
  233.6 6.0 %copy-start.4 = (bf16[256,8,128]{0,2,1:T(8,128)(2,1)S(1)}, bf16[256,8,128]{0,2,1:T(8,128)(2,1)}, u32[]{:S(2)}) copy-start(bf16[256,8,128]{0,2,1:T(8,128)(2,1)} %copy.20) | copy-start | bytes 1572868

commit v4 on v3

--- a/solution.py
+++ b/solution.py
@@ -37,7 +37,7 @@
     return y * 8 + z * 2 + c
 
 
-def greet(y, z, c):
+def greet(y, z, c, *more):
     barrier = pltpu.get_barrier_semaphore()
     for other in (
         index_of(up(y), z, c),
@@ -45,9 +45,9 @@
         index_of(y, up(z), c),
         index_of(y, down(z), c),
         index_of(y, z, 1 - c),
-    ):
+    ) + more:
         pl.semaphore_signal(barrier, inc=1, device_id={"seq": other}, device_id_type=MESH)
-    pl.semaphore_wait(barrier, 5)
+    pl.semaphore_wait(barrier, 5 + len(more))
 
 
 def dot_t(a, b):
@@ -107,15 +107,20 @@
 
 
 def core_kernel(
-    ids, first, second, own, q_ref, g_ref,
-    att_ref, dq_ref, out, tab, landed,
+    ids, first, second, enc, w_key, w_value, queries, cotangents,
+    att_out, dq_out, out, tab, landed,
     table_even, table_odd, ck, cv, acc, give_even, give_odd, got_even, got_odd,
-    r1, r2, r3, r4, send_sem, recv_sem, back_send, back_recv, own_sem, load_sem,
+    own, q_buf, g_buf, att_buf, dq_buf, r1, r2, r3, r4,
+    send_sem, recv_sem, back_send, back_recv, own_sem, load_sem,
+    enc_sem, w_sem, row_sem, rim_send, rim_recv,
 ):
     y, z, c = place()
-    greet(y, z, c)
+    me = index_of(y, z, c)
+    count = 2 * RING * RING
+    ahead, behind = lax.rem(me + 1, count), lax.rem(me + count - 1, count)
     pairs = own.shape[0] // 2
-    spans = q_ref.shape[0] // SPAN
+    tokens = queries.shape[0]
+    spans = tokens // SPAN
     reads = 2 * spans
     group = max(n for n in range(1, 8) if spans % n == 0)
     sibling = index_of(y, z, 1 - c)
@@ -123,8 +128,123 @@
     held = (table_even, table_odd)
     give = (give_even, give_odd)
     got = (got_even, got_odd)
+    weights = (w_key, w_value)
+    body, head_rows, tail_rows = pl.ds(0, tokens), pl.ds(0, SPAN), pl.ds(tokens, SPAN)
+
+    def enc_copy(piece):
+        at = (lax.div(piece, 8), lax.rem(lax.div(piece, 2), RING), lax.rem(piece, 2))
+        return pltpu.make_async_copy(
+            enc.at[:, pl.ds(pl.multiple_of(piece * HD, HD), HD)], got_even.at[at], enc_sem.at[piece]
+        )
+
+    def weight_copy(h, kv):
+        cols = pl.ds(pl.multiple_of(h * HD, HD), HD)
+        return pltpu.make_async_copy(
+            weights[kv].at[:, :, :, cols], acc.at[h, :, :, kv], w_sem.at[h, kv]
+        )
+
+    def for_pieces(action):
+        def one(piece, carry):
+            action(enc_copy(piece))
+            return carry
+
+        lax.fori_loop(0, enc_sem.shape[0], one, 0)
+
+    for_pieces(lambda copy: copy.start())
+    for h in (0, 1):
+        for kv in (0, 1):
+            weight_copy(h, kv).start()
+    greet(y, z, c, ahead, behind)
     ck[reads] = jnp.zeros(ck.shape[1:], jnp.float32)
     cv[reads] = jnp.zeros(cv.shape[1:], jnp.float32)
+    for_pieces(lambda copy: copy.wait())
+
+    def row_copies():
+        return (
+            pltpu.make_async_copy(queries, q_buf.at[body], row_sem.at[0]),
+            pltpu.make_async_copy(cotangents, g_buf.at[body], row_sem.at[1]),
+        )
+
+    def result_copies():
+        return (
+            pltpu.make_async_copy(att_buf.at[body], att_out, row_sem.at[2]),
+            pltpu.make_async_copy(dq_buf.at[body], dq_out, row_sem.at[3]),
+        )
+
+    def rim_move(kind):
+        src, dst, to = (
+            (queries.at[head_rows], q_buf.at[tail_rows], behind),
+            (cotangents.at[head_rows], g_buf.at[tail_rows], behind),
+            (att_buf.at[tail_rows], att_buf.at[head_rows], ahead),
+            (dq_buf.at[tail_rows], dq_buf.at[head_rows], ahead),
+        )[kind]
+        return pltpu.make_async_remote_copy(
+            src_ref=src,
+            dst_ref=dst,
+            send_sem=rim_send.at[kind],
+            recv_sem=rim_recv.at[kind],
+            device_id={"seq": to},
+            device_id_type=MESH,
+        )
+
+    def by_blocks(refs, blend):
+        strip = 256
+        line = lax.broadcasted_iota(jnp.int32, (SPAN, strip), 0)
+
+        def one(block, carry):
+            for ref in refs:
+                for start in range(0, ref.shape[1], strip):
+                    blend(ref, block, pl.ds(start, strip), line)
+            return carry
+
+        lax.fori_loop(0, spans, one, 0)
+
+    def rows_start():
+        for copy in row_copies():
+            copy.start()
+        rim_move(0).start()
+        rim_move(1).start()
+
+    def rows_in():
+        for kind, copy in enumerate(row_copies()):
+            copy.wait()
+            rim_move(kind).wait()
+
+        @pl.when(me == count - 1)
+        def _():
+            for ref in (q_buf, g_buf):
+                ref[tail_rows] = jnp.zeros((SPAN, ref.shape[1]), jnp.bfloat16)
+
+        def blend(ref, block, cols, line):
+            at = pl.multiple_of(block * SPAN, SPAN)
+            before = wide(ref[pl.ds(at + SPAN - 16, 16), cols])[15:16]
+            after = pltpu.roll(wide(ref[pl.ds(at + SPAN, SPAN), cols]), 1, 0)
+            ref[pl.ds(at, SPAN), cols] = jnp.where(line == 0, before, after).astype(jnp.bfloat16)
+
+        by_blocks((q_buf, g_buf), blend)
+
+    def tail_out():
+        rim_move(2).start()
+        rim_move(3).start()
+
+    def rows_out():
+        rim_move(2).wait()
+        rim_move(3).wait()
+
+        @pl.when(me == 0)
+        def _():
+            for ref in (att_buf, dq_buf):
+                ref[head_rows] = jnp.zeros((SPAN, ref.shape[1]), jnp.bfloat16)
+
+        def blend(ref, block, cols, line):
+            at = pl.multiple_of(block * SPAN, SPAN)
+            here = pltpu.roll(wide(ref[pl.ds(at, SPAN), cols]), SPAN - 1, 0)
+            after = wide(ref[pl.ds(at + SPAN, 16), cols])[0:1]
+            ref[pl.ds(at, SPAN), cols] = jnp.where(line == SPAN - 1, after, here).astype(jnp.bfloat16)
+
+        by_blocks((att_buf, dq_buf), blend)
+        for copy in result_copies():
+            copy.start()
 
     class Head:
         def __init__(self, h, parity):
@@ -209,6 +329,30 @@
                 device_id_type=MESH,
             )
 
+    def project(t):
+        for kv in (0, 1):
+            weight_copy(t.h, kv).wait()
+
+        @pl.when(t.h + 2 < 2 * pairs)
+        def _():
+            for kv in (0, 1):
+                weight_copy(t.h + 2, kv).start()
+
+        deep = [(a, b) for a in range(RING) for b in range(RING)]
+
+        def one(s, carry):
+            lines = pl.ds(pl.multiple_of(s * NBR_LEN, NBR_LEN), NBR_LEN)
+            left = jnp.concatenate([got_even[a, b, k, lines] for a, b in deep for k in (0, 1)], axis=1)
+            right = jnp.concatenate(
+                [jnp.concatenate([acc[t.h, a, b, kv] for kv in (0, 1)], axis=1) for a, b in deep], axis=0
+            )
+            rows = jnp.dot(left, right, preferred_element_type=jnp.float32).astype(jnp.bfloat16)
+            for kv in (0, 1):
+                own[t.h, kv, s] = rows[:, kv * HD : (kv + 1) * HD]
+            return carry
+
+        lax.fori_loop(0, 2, one, 0)
+
     def own_out(t):
         t.mine().start()
         t.out_move(0).start()
@@ -263,14 +407,15 @@
         def some(i, carry):
             spots = [i * group + u for u in range(group)]
             rows = [pl.ds(pl.multiple_of(s * SPAN, SPAN), SPAN) for s in spots]
-            qs, gs = [q_ref[r, cols] for r in rows], [g_ref[r, cols] for r in rows]
+            qs, gs = [q_buf[r, cols] for r in rows], [g_buf[r, cols] for r in rows]
             picks = [[ids[2 * s + j] for j in (0, 1)] for s in spots]
             keys = [[pick(n, 0) for n in two] for two in picks]
             values = [[pick(n, 1) for n in two] for two in picks]
             merged, d_query, d_keys, d_values = spans_math(qs, gs, keys, values)
             for u, s in enumerate(spots):
-                att_ref[rows[u], cols] = merged[u].astype(jnp.bfloat16)
-                dq_ref[rows[u], cols] = d_query[u].astype(jnp.bfloat16)
+                put = pl.ds(pl.multiple_of((s + 1) * SPAN, SPAN), SPAN)
+                att_buf[put, cols] = merged[u].astype(jnp.bfloat16)
+                dq_buf[put, cols] = d_query[u].astype(jnp.bfloat16)
                 for j in (0, 1):
                     ck[2 * s + j] = d_keys[u][j * NBR_LEN : (j + 1) * NBR_LEN]
                     cv[2 * s + j] = d_values[u][j * NBR_LEN : (j + 1) * NBR_LEN]
@@ -354,6 +499,7 @@
             t.back_move(kind).wait_send()
 
     stages = (
+        (0, project),
         (0, own_out),
         (1, block_on),
         (2, band_out),
@@ -369,6 +515,8 @@
         (6, sum_sibling),
     )
 
+    once = {0: rows_start, 3: rows_in, pairs + 4: tail_out, pairs + 5: rows_out}
+
     def step(i, carry):
         for lag, stage in stages:
 
@@ -377,15 +525,20 @@
                 for parity in (0, 1):
                     stage(Head(2 * (i - lag) + parity, parity))
 
+        for when, act in once.items():
+            pl.when(i == when)(act)
         return carry
 
     lax.fori_loop(0, pairs + max(lag for lag, _ in stages), step, 0)
-
-
-def core(ids, first, second, own, query_shift, grad_shift):
-    rows, width = query_shift.shape
-    heads, reads = own.shape[0], ids.shape[0]
-    rest = own.shape[1:]
+    for copy in result_copies():
+        copy.wait()
+
+
+def core(ids, first, second, enc, w_key, w_value, queries, cotangents):
+    rows, width = queries.shape
+    depth = enc.shape[1]
+    heads, reads = width // HD, ids.shape[0]
+    rest = (2, 2, NBR_LEN, HD)
     tail = (2, 2 * NBR_LEN, HD)
     bf16, f32 = jnp.bfloat16, jnp.float32
     in_vmem = pl.BlockSpec(memory_space=pltpu.VMEM)
@@ -393,10 +546,11 @@
     anywhere = pl.BlockSpec(memory_space=pl.ANY)
     band = (RING, RING) + tail
     dma = pltpu.SemaphoreType.DMA
+    folded = (RING, RING, depth // (RING * RING), width)
     return pl.pallas_call(
         core_kernel,
-        in_specs=[in_smem, in_smem, in_smem, anywhere, in_vmem, in_vmem],
-        out_specs=[in_vmem, in_vmem, in_vmem, anywhere, anywhere],
+        in_specs=[in_smem] * 3 + [anywhere] * 5,
+        out_specs=[anywhere, anywhere, in_vmem, anywhere, anywhere],
         out_shape=[
             jax.ShapeDtypeStruct((rows, width), bf16),
             jax.ShapeDtypeStruct((rows, width), bf16),
@@ -414,6 +568,11 @@
             pltpu.VMEM(band, bf16),
             pltpu.VMEM(band, bf16),
             pltpu.VMEM(band, bf16),
+            pltpu.VMEM((heads,) + rest, bf16),
+            pltpu.VMEM((rows + SPAN, width), bf16),
+            pltpu.VMEM((rows + SPAN, width), bf16),
+            pltpu.VMEM((rows + SPAN, width), bf16),
+            pltpu.VMEM((rows + SPAN, width), bf16),
             pltpu.VMEM((heads, 2, RING) + tail[1:], bf16),
             pltpu.VMEM((heads, 2, RING) + tail, bf16),
             pltpu.VMEM((heads, 2) + tail[1:], bf16),
@@ -424,27 +583,53 @@
             dma((heads, 9)),
             dma((heads,)),
             dma((heads, 2)),
+            dma((depth // HD,)),
+            dma((heads, 2)),
+            dma((4,)),
+            dma((4,)),
+            dma((4,)),
         ],
         compiler_params=pltpu.CompilerParams(
             collective_id=0, has_side_effects=True, vmem_limit_bytes=63 * MIB
         ),
         name="core",
-    )(ids, first, second, own, query_shift, grad_shift)
-
-
-def enc_kernel(part, out, s1, s2, r1, r2, send_sem, recv_sem):
+    )(ids, first, second, enc, w_key.reshape(folded), w_value.reshape(folded), queries, cotangents)
+
+
+def final_kernel(
+    grads, w_key, w_value, out, held, wide_right, wide_left, s1, s2, r1, r2, send_sem, recv_sem, w_sem
+):
     x = lax.axis_index("enc")
     right, left = up(x), down(x)
+    order = (across(x), right, left, x)
+    weights = (w_key, w_value)
+    heads = grads.shape[0]
+
+    def weight_copy(k, kv):
+        return pltpu.make_async_copy(weights[kv].at[order[k]], held.at[k, kv], w_sem.at[k, kv])
+
+    for k in range(RING):
+        for kv in (0, 1):
+            weight_copy(k, kv).start()
     barrier = pltpu.get_barrier_semaphore()
     for other in (right, left):
         pl.semaphore_signal(barrier, inc=1, device_id={"enc": other}, device_id_type=MESH)
     pl.semaphore_wait(barrier, 2)
-    rows = part.shape[0]
+    rows, width = out.shape
     half = rows // 2
-    width = out.shape[1]
-
-    def cols(t):
-        return pl.ds(pl.multiple_of(t * width, width), width)
+    strip = 256
+    lhs = [jnp.concatenate([grads[h, kv] for h in range(heads)], axis=1) for kv in (0, 1)]
+
+    def product(k, put):
+        for kv in (0, 1):
+            weight_copy(k, kv).wait()
+
+        def one(n, carry):
+            lines = pl.ds(pl.multiple_of(n * strip, strip), strip)
+            put(lines, sum(dot_t(lhs[kv], held[k, kv, lines, :]) for kv in (0, 1)))
+            return carry
+
+        lax.fori_loop(0, width // strip, one, 0)
 
     def remote(kind, src, dst, to):
         return pltpu.make_async_remote_copy(
@@ -462,59 +647,79 @@
         remote(2, s2.at[0], r2.at[0], right),
         remote(3, s2.at[1], r2.at[1], left),
     ]
-    far = cols(across(x))
-    s1[0] = part[:half, far].astype(jnp.bfloat16)
+
+    def put_far(cols, part):
+        s1[0, :, cols] = part[:half].astype(jnp.bfloat16)
+        s1[1, :, cols] = part[half:].astype(jnp.bfloat16)
+
+    def put_right(cols, part):
+        wide_right[:, cols] = part[:half]
+        s2[0, pl.ds(half, half), cols] = part[half:].astype(jnp.bfloat16)
+
+    def put_left(cols, part):
+        s2[1, pl.ds(0, half), cols] = part[:half].astype(jnp.bfloat16)
+        wide_left[:, cols] = part[half:]
+
+    product(0, put_far)
     moves[0].start()
-    s1[1] = part[half:, far].astype(jnp.bfloat16)
     moves[1].start()
-    s2[0, half:] = part[half:, cols(right)].astype(jnp.bfloat16)
-    s2[1, :half] = part[:half, cols(left)].astype(jnp.bfloat16)
+    product(1, put_right)
+    product(2, put_left)
     moves[0].wait_recv()
-    s2[0, :half] = (part[:half, cols(right)] + wide(r1[0])).astype(jnp.bfloat16)
+    s2[0, :half] = (wide_right[...] + wide(r1[0])).astype(jnp.bfloat16)
     moves[2].start()
     moves[1].wait_recv()
-    s2[1, half:] = (part[half:, cols(left)] + wide(r1[1])).astype(jnp.bfloat16)
+    s2[1, half:] = (wide_left[...] + wide(r1[1])).astype(jnp.bfloat16)
     moves[3].start()
+
+    def put_mine(cols, part):
+        wide_right[:, cols] = part[:half]
+        wide_left[:, cols] = part[half:]
+
+    product(3, put_mine)
     moves[2].wait_recv()
     moves[3].wait_recv()
-    out[...] = (part[:, cols(x)] + wide(r2[0]) + wide(r2[1])).astype(jnp.bfloat16)
+    for part, lines in ((wide_right, pl.ds(0, half)), (wide_left, pl.ds(half, half))):
+        total = part[...] + wide(r2[0, lines]) + wide(r2[1, lines])
+        out[lines] = total.astype(jnp.bfloat16)
     for move in moves:
         move.wait_send()
 
 
-def scatter_enc(part):
-    rows, width = part.shape[0], part.shape[1] // RING
+def final(grads, w_key, w_value):
+    rows, width = grads.shape[2], w_key.shape[1]
     half = rows // 2
+    bf16 = jnp.bfloat16
+    blocks = (RING, w_key.shape[0] // RING, width)
+    in_vmem = pl.BlockSpec(memory_space=pltpu.VMEM)
+    anywhere = pl.BlockSpec(memory_space=pl.ANY)
     return pl.pallas_call(
-        enc_kernel,
-        out_shape=jax.ShapeDtypeStruct((rows, width), jnp.bfloat16),
-        in_specs=[pl.BlockSpec(memory_space=pltpu.VMEM)],
-        out_specs=pl.BlockSpec(memory_space=pltpu.VMEM),
+        final_kernel,
+        out_shape=jax.ShapeDtypeStruct((rows, blocks[1]), bf16),
+        in_specs=[in_vmem, anywhere, anywhere],
+        out_specs=in_vmem,
         scratch_shapes=[
-            pltpu.VMEM((2, half, width), jnp.bfloat16),
-            pltpu.VMEM((2, rows, width), jnp.bfloat16),
-            pltpu.VMEM((2, half, width), jnp.bfloat16),
-            pltpu.VMEM((2, rows, width), jnp.bfloat16),
+            pltpu.VMEM((RING, 2) + blocks[1:], bf16),
+            pltpu.VMEM((half, blocks[1]), jnp.float32),
+            pltpu.VMEM((half, blocks[1]), jnp.float32),
+            pltpu.VMEM((2, half, blocks[1]), bf16),
+            pltpu.VMEM((2, rows, blocks[1]), bf16),
+            pltpu.VMEM((2, half, blocks[1]), bf16),
+            pltpu.VMEM((2, rows, blocks[1]), bf16),
             pltpu.SemaphoreType.DMA((4,)),
             pltpu.SemaphoreType.DMA((4,)),
+            pltpu.SemaphoreType.DMA((RING, 2)),
         ],
         compiler_params=pltpu.CompilerParams(
-            collective_id=2, has_side_effects=True, vmem_limit_bytes=32 * MIB
+            collective_id=1, has_side_effects=True, vmem_limit_bytes=48 * MIB
         ),
-        name="scatter_enc",
-    )(part)
-
-
-def shifted(value, axis, steps):
-    count = lax.axis_size(axis)
-    first, last = (max(0, -steps), min(count, count - steps))
-    return lax.ppermute(value, axis, [(source, source + steps) for source in range(first, last)])
+        name="final",
+    )(grads, w_key.reshape(blocks), w_value.reshape(blocks))
 
 
 def per_device(queries, d_attended, encodings, w_key, w_value, neighbour_owner, neighbour_slot):
     tok_rows, feat_width = queries.shape
     heads = feat_width // HD
-    margin = SPAN - 1
     owned = encodings.shape[0]
     owners = lax.axis_size("seq")
     reads = 2 * (tok_rows // SPAN)
@@ -526,31 +731,11 @@
     last = jnp.max(jnp.where(hit, order, -1), axis=1)
     second = jnp.where(last > first, last, reads)
 
-    rim_rows = shifted(jnp.stack([queries[:margin], d_attended[:margin]]), "seq", -1)
-    query_shift = jnp.concatenate([queries[margin:], rim_rows[0]], axis=0)
-    grad_shift = jnp.concatenate([d_attended[margin:], rim_rows[1]], axis=0)
-
     enc_flat = encodings.reshape(owned * NBR_LEN, encodings.shape[2])
-    tables = [
-        jnp.dot(enc_flat, w, preferred_element_type=jnp.float32)
-        .astype(jnp.bfloat16)
-        .reshape(owned, NBR_LEN, heads, HD)
-        .transpose(2, 0, 1, 3)
-        for w in (w_key, w_value)
-    ]
-    attended_shift, dq_shift, grads, _, _ = core(
-        ids, first, second, jnp.stack(tables, axis=1), query_shift, grad_shift
+    attended, d_queries, grads, _, _ = core(
+        ids, first, second, enc_flat, w_key, w_value, queries, d_attended
     )
-    attended_tail = shifted(attended_shift[tok_rows - margin :], "seq", 1)
-    query_tail = shifted(dq_shift[tok_rows - margin :], "seq", 1)
-    contract = (((1,), (1,)), ((), ()))
-    part = 0.0
-    for kv, w in enumerate((w_key, w_value)):
-        rows = grads[:, kv].transpose(1, 0, 2).reshape(owned * NBR_LEN, feat_width)
-        part = part + lax.dot_general(rows, w, contract, preferred_element_type=jnp.float32)
-    d_encodings = scatter_enc(part).reshape(owned, NBR_LEN, feat_width)
-    attended = jnp.concatenate([attended_tail, attended_shift[: tok_rows - margin]], axis=0)
-    d_queries = jnp.concatenate([query_tail, dq_shift[: tok_rows - margin]], axis=0)
+    d_encodings = final(grads, w_key, w_value).reshape(owned, NBR_LEN, feat_width)
     return (attended, d_queries, d_encodings)
 
 

time: 273 us -> 231 us (0.85)
  matrix products: 24.1 us -> 0 us
  starting transfers between devices: 13.1 us -> 0 us
  Pallas kernels: 209 us -> 221 us
  other arithmetic: 10.6 us -> 1.3 us
  local copies, waits for them, and re-layouts: 14.1 us -> 5.59 us
    dot_general x4 -> x0, matrix products: 24.1 us -> none  [the longest x2 12.3 us: per_device(): jnp.dot(enc_flat, w, preferred_element_type=jnp.float32)]
    ppermute x3 -> x0, starting transfers between devices: 13.1 us -> none  [shifted(): lax.ppermute(value, axis, [(source, source + steps) for source in range(f...]
    pallas_call x2, Pallas kernels: 209 us -> 221 us  [the longest x1 199 us: core(): pl.pallas_call(core_kernel, in_specs=[in_smem] * 3 + [anywhere] * 5, out_...]
    concatenate x4 -> x0, other arithmetic: 8.11 us -> none  [the longest x1 2.6 us: per_device(): jnp.concatenate([query_tail, dq_shift[:tok_rows - margin]], axis=0)]
    transpose x3 -> x0, local copies, waits for them, and re-layouts: 5.13 us -> none  [per_device(): rows = grads[:, kv].transpose(1, 0, 2).reshape(owned * NBR_LEN, feat_width)]
    slice x6 -> x0, local copies, waits for them, and re-layouts: 5 us -> none  [the longest x1 1.71 us: per_device(): attended_tail = shifted(attended_shift[tok_rows - margin:], 'seq', 1)]
    unnamed x19 -> x13, local copies, waits for them, and re-layouts: 2.54 us -> 5.41 us
  transfers between devices with their start and end apart: 3 -> 0, of which waited for: 0 -> 0; matrix products, arithmetic and copies ran while one was open for 12% -> 0% of each run, Pallas kernels for 7% -> 0%
where the time goes in v4:
time: 231 us; the launch traced here: 229 us
  Pallas kernels  221 us (96%)
  local copies, waits for them, and re-layouts  5.59 us (2%)
    pallas_call x1, Pallas kernels, core(): pl.pallas_call(core_kernel, in_specs=[in_smem] * 3 + [anywhere] * 5, out_...  199 us
    pallas_call x1, Pallas kernels, final(): pl.pallas_call(final_kernel, out_shape=jax.ShapeDtypeStruct((rows, blocks...  22.8 us
    unnamed x13, local copies, waits for them, and re-layouts  5.41 us

profile of v4, /device:TPU:1, one launch (start us, length us, event | category | flops | bytes accessed | tf_op | source)
XLA Modules:
  0.0 229.0 jit_solution(10496038631018268918)
XLA Ops:
  0.6 0.7 multiply_add_fusion
  1.3 0.1 copy.12
  1.4 0.1 reshape.28.ids
  1.5 0.0 copy-start.3
  1.5 0.1 select_reduce_fusion
  1.6 0.0 copy-start.4
  1.6 0.5 compare_select_fusion.second
  2.1 0.0 copy-done.3
  2.1 0.0 copy-done.4
  2.1 198.6 %core.1 = (bf16[896,1024]{1,0:T(8,128)(2,1)}, bf16[896,1024]{1,0:T(8,128)(2,1)}, bf16[8,2,256,128]{3,2,1,0:T(8,128)(2,1)}, bf16[8,4,4,2,2,2,128,128]{7,6,5,4,3,2...) custom-call(s32[28]{0:T(128)} %copy-done.3, s32[64]{0:T(128)} %copy-done.4, s32[64]{0:T(128)} %compare_select_fusion.second, ...), custom_call_target="tpu_custom_call" | custom-call | tf_op jit(solution)/shard_map/core/pallas_call | solution.py:550
  200.8 0.0 copy-start
  200.8 1.2 copy-done
  202.0 0.0 copy-start.2
  202.0 22.8 %final.1 = bf16[256,1024]{1,0:T(8,128)(2,1)S(1)} custom-call(bf16[8,2,256,128]{3,2,1,0:T(8,128)(2,1)S(1)} %copy-done, bf16[4,1024,1024]{2,1,0:T(8,128)(2,1)} %bitcast.8, bf16[4,1024,1024]{2,1,0:T(8,128)(2,1)} %bitcast.10), custom_call_target="tpu_custom_call" | custom-call | tf_op jit(solution)/shard_map/final/pallas_call | solution.py:696
  224.8 0.0 copy-done.2
  224.8 0.0 copy-start.1
  224.8 1.2 copy.16
  226.0 0.9 copy-done.1
  227.0 1.2 copy.17
  228.2 0.8 copy.18
Async XLA Ops:
  1.5 0.6 copy-start.3
  1.6 0.5 copy-start.4
  200.8 1.2 copy-start
  202.0 22.8 %copy-start.2 = (bf16[896,1024]{1,0:T(8,128)(2,1)S(1)}, bf16[896,1024]{1,0:T(8,128)(2,1)}, u32[]{:S(2)}) copy-start(bf16[896,1024]{1,0:T(8,128)(2,1)} %get-tuple-element.14) | copy-start | bytes 5505028
  224.8 2.2 copy-start.1

commit v5 on v4

--- a/solution.py
+++ b/solution.py
@@ -37,17 +37,19 @@
     return y * 8 + z * 2 + c
 
 
-def greet(y, z, c, *more):
+def greet(y, z, c, seq_more, enc_more):
     barrier = pltpu.get_barrier_semaphore()
-    for other in (
+    near = (
         index_of(up(y), z, c),
         index_of(down(y), z, c),
         index_of(y, up(z), c),
         index_of(y, down(z), c),
         index_of(y, z, 1 - c),
-    ) + more:
-        pl.semaphore_signal(barrier, inc=1, device_id={"seq": other}, device_id_type=MESH)
-    pl.semaphore_wait(barrier, 5 + len(more))
+    )
+    partners = [{"seq": other} for other in near + seq_more] + [{"enc": other} for other in enc_more]
+    for partner in partners:
+        pl.semaphore_signal(barrier, inc=1, device_id=partner, device_id_type=MESH)
+    pl.semaphore_wait(barrier, len(partners))
 
 
 def dot_t(a, b):
@@ -108,17 +110,19 @@
 
 def core_kernel(
     ids, first, second, enc, w_key, w_value, queries, cotangents,
-    att_out, dq_out, out, tab, landed,
+    att_out, dq_out, enc_out, tab, landed,
     table_even, table_odd, ck, cv, acc, give_even, give_odd, got_even, got_odd,
-    own, q_buf, g_buf, att_buf, dq_buf, r1, r2, r3, r4,
+    own, q_buf, g_buf, att_buf, dq_buf, r1, r2, r3, r4, e1, e2,
     send_sem, recv_sem, back_send, back_recv, own_sem, load_sem,
-    enc_sem, w_sem, row_sem, rim_send, rim_recv,
+    enc_sem, w_sem, row_sem, rim_send, rim_recv, block_sem, enc_send, enc_recv,
 ):
+    x = lax.axis_index("enc")
+    right, left = up(x), down(x)
     y, z, c = place()
     me = index_of(y, z, c)
     count = 2 * RING * RING
     ahead, behind = lax.rem(me + 1, count), lax.rem(me + count - 1, count)
-    pairs = own.shape[0] // 2
+    heads = own.shape[0]
     tokens = queries.shape[0]
     spans = tokens // SPAN
     reads = 2 * spans
@@ -154,7 +158,7 @@
     for h in (0, 1):
         for kv in (0, 1):
             weight_copy(h, kv).start()
-    greet(y, z, c, ahead, behind)
+    greet(y, z, c, (ahead, behind), (right, left))
     ck[reads] = jnp.zeros(ck.shape[1:], jnp.float32)
     cv[reads] = jnp.zeros(cv.shape[1:], jnp.float32)
     for_pieces(lambda copy: copy.wait())
@@ -247,8 +251,9 @@
             copy.start()
 
     class Head:
-        def __init__(self, h, parity):
-            self.h, self.parity = h, parity
+        def __init__(self, h, parity, slots=(0, 1)):
+            self.h, self.parity, self.slots = h, parity, slots
+            self.lines = pl.ds(slots[0] * NBR_LEN, len(slots) * NBR_LEN)
             self.f, self.g = (y, z) if parity == 0 else (z, y)
 
         def dev(self, a, b):
@@ -308,23 +313,25 @@
             )
 
         def back_move(self, kind):
-            f, g, dev, h = self.f, self.g, self.dev, self.h
+            f, g, dev, h, spot = self.f, self.g, self.dev, self.h, self.spot
+            here = self.lines
             src, dst, to = (
                 lambda: (give[self.parity], landed.at[h], sibling),
-                lambda: (acc.at[self.spot(every, across(g)) + (0,)], r1.at[h, 0], dev(f, up(g))),
-                lambda: (acc.at[self.spot(every, across(g)) + (1,)], r1.at[h, 1], dev(f, down(g))),
-                lambda: (acc.at[self.spot(every, up(g))], r2.at[h, 0], dev(f, up(g))),
-                lambda: (acc.at[self.spot(every, down(g))], r2.at[h, 1], dev(f, down(g))),
-                lambda: (acc.at[self.spot(across(f), g) + (0,)], r3.at[h, 0], dev(up(f), g)),
-                lambda: (acc.at[self.spot(across(f), g) + (1,)], r3.at[h, 1], dev(down(f), g)),
-                lambda: (acc.at[self.spot(up(f), g)], r4.at[h, 0], dev(up(f), g)),
-                lambda: (acc.at[self.spot(down(f), g)], r4.at[h, 1], dev(down(f), g)),
+                lambda: (acc.at[spot(every, across(g)) + (0, here)], r1.at[h, 0, :, here], dev(f, up(g))),
+                lambda: (acc.at[spot(every, across(g)) + (1, here)], r1.at[h, 1, :, here], dev(f, down(g))),
+                lambda: (acc.at[spot(every, up(g)) + (every, here)], r2.at[h, 0, :, :, here], dev(f, up(g))),
+                lambda: (acc.at[spot(every, down(g)) + (every, here)], r2.at[h, 1, :, :, here], dev(f, down(g))),
+                lambda: (acc.at[spot(across(f), g) + (0, here)], r3.at[h, 0, here], dev(up(f), g)),
+                lambda: (acc.at[spot(across(f), g) + (1, here)], r3.at[h, 1, here], dev(down(f), g)),
+                lambda: (acc.at[spot(up(f), g) + (every, here)], r4.at[h, 0, :, here], dev(up(f), g)),
+                lambda: (acc.at[spot(down(f), g) + (every, here)], r4.at[h, 1, :, here], dev(down(f), g)),
             )[kind]()
+            place_of = 0 if kind == 0 else self.slots[0] * 8 + kind
             return pltpu.make_async_remote_copy(
                 src_ref=src,
                 dst_ref=dst,
-                send_sem=back_send.at[h, kind],
-                recv_sem=back_recv.at[h, kind],
+                send_sem=back_send.at[h, place_of],
+                recv_sem=back_recv.at[h, place_of],
                 device_id={"seq": to},
                 device_id_type=MESH,
             )
@@ -333,7 +340,7 @@
         for kv in (0, 1):
             weight_copy(t.h, kv).wait()
 
-        @pl.when(t.h + 2 < 2 * pairs)
+        @pl.when(t.h + 2 < heads)
         def _():
             for kv in (0, 1):
                 weight_copy(t.h + 2, kv).start()
@@ -354,6 +361,7 @@
         lax.fori_loop(0, 2, one, 0)
 
     def own_out(t):
+        project(t)
         t.mine().start()
         t.out_move(0).start()
         t.out_move(1).start()
@@ -451,6 +459,8 @@
             return carry
 
         lax.fori_loop(0, RING * RING, add, 0)
+
+    def halves_out(t):
         t.back_move(1).start()
         t.back_move(2).start()
 
@@ -459,8 +469,8 @@
             t.back_move(kind).wait_recv()
 
             def add(a, carry):
-                at = t.spot(a, toward) + (half,)
-                acc[at] = acc[at] + r1[t.h, half, a]
+                at = t.spot(a, toward) + (half, t.lines)
+                acc[at] = acc[at] + r1[t.h, half, a, t.lines]
                 return carry
 
             lax.fori_loop(0, RING, add, 0)
@@ -472,8 +482,8 @@
 
         def add(a, carry):
             for kv in (0, 1):
-                at = t.spot(a, t.g) + (kv,)
-                total = wide(acc[at]) + wide(r2[t.h, 0, a, kv]) + wide(r2[t.h, 1, a, kv])
+                at = t.spot(a, t.g) + (kv, t.lines)
+                total = wide(acc[at]) + wide(r2[t.h, 0, a, kv, t.lines]) + wide(r2[t.h, 1, a, kv, t.lines])
                 acc[at] = total.astype(jnp.bfloat16)
             return carry
 
@@ -484,52 +494,234 @@
     def sum_block_half(t):
         for half, (kind, toward) in enumerate(((5, up(t.f)), (6, down(t.f)))):
             t.back_move(kind).wait_recv()
-            at = t.spot(toward, t.g) + (half,)
-            acc[at] = acc[at] + r3[t.h, half]
+            at = t.spot(toward, t.g) + (half, t.lines)
+            acc[at] = acc[at] + r3[t.h, half, t.lines]
             t.back_move(7 + half).start()
 
     def sum_block(t):
         t.back_move(7).wait_recv()
         t.back_move(8).wait_recv()
         for kv in (0, 1):
-            total = wide(acc[t.spot(t.f, t.g) + (kv,)])
-            total = total + wide(r4[t.h, 0, kv]) + wide(r4[t.h, 1, kv])
-            out[t.h, kv] = total.astype(jnp.bfloat16)
+            for slot in t.slots:
+                lines = pl.ds(slot * NBR_LEN, NBR_LEN)
+                total = wide(acc[t.spot(t.f, t.g) + (kv, lines)])
+                total = total + wide(r4[t.h, 0, kv, lines]) + wide(r4[t.h, 1, kv, lines])
+                own[t.h, kv, slot] = total.astype(jnp.bfloat16)
         for kind in range(1, 9):
             t.back_move(kind).wait_send()
 
-    stages = (
-        (0, project),
+    pairs = heads // 2
+    split = (pairs - 2, pairs - 1)
+    sums = (ck, cv)
+
+    def pair_copies(pair, action):
+        for n in (0, 1):
+            cols = pl.ds((2 * pair + n) * HD, HD)
+            for core in (0, 1):
+                for kv in (0, 1):
+                    action(
+                        pltpu.make_async_copy(
+                            weights[kv].at[:, :, pl.ds(core * HD, HD), cols],
+                            held[pair % 2].at[:, :, core, kv, n],
+                            block_sem.at[pair, 4 * n + 2 * core + kv],
+                        )
+                    )
+
+    def pair_start(*which):
+        for pair in which:
+            pair_copies(pair, lambda copy: copy.start())
+
+    deep = [(kv, n) for kv in (0, 1) for n in (0, 1)]
+
+    def rows_of(pair, slot):
+        return jnp.concatenate([own[2 * pair + n, kv, slot] for kv, n in deep], axis=1)
+
+    def weights_of(pair, t, a):
+        table = held[pair % 2]
+        return jnp.concatenate(
+            [jnp.concatenate([table[t, a, core, kv, n] for kv, n in deep], axis=1) for core in (0, 1)],
+            axis=0,
+        )
+
+    def gather_pair(pair):
+        pair_copies(pair, lambda copy: copy.wait())
+        lhs = jnp.concatenate([rows_of(pair, slot) for slot in (0, 1)], axis=0)
+
+        def one(m, carry):
+            t, a = lax.div(m, RING), lax.rem(m, RING)
+            part = dot_t(lhs, weights_of(pair, t, a))
+            for slot in (0, 1):
+                for core in (0, 1):
+                    at = 8 * t + 2 * a + core
+                    piece = part[slot * NBR_LEN : (slot + 1) * NBR_LEN, core * HD : (core + 1) * HD]
+                    sums[slot][at] = piece if pair == 0 else sums[slot][at] + piece
+            return carry
+
+        lax.fori_loop(0, RING * RING, one, 0)
+
+    def product(slot, t, put):
+        lhs = [rows_of(pair, slot) for pair in split]
+
+        def one(a, carry):
+            part = sum(dot_t(rows, weights_of(pair, t, a)) for rows, pair in zip(lhs, split))
+            for core in (0, 1):
+                at = 8 * t + 2 * a + core
+                put(a, core, at, sums[slot][at] + part[:, core * HD : (core + 1) * HD])
+            return carry
+
+        lax.fori_loop(0, RING, one, 0)
+
+    half = NBR_LEN // 2
+    low, high, whole = pl.ds(0, half), pl.ds(half, half), pl.ds(0, NBR_LEN)
+
+    def enc_move(slot, kind):
+        src, dst, to = (
+            lambda: (give[slot].at[0, :, :, low], e1.at[slot, 0], right),
+            lambda: (give[slot].at[1, :, :, low], e1.at[slot, 1], left),
+            lambda: (give[slot].at[2, :, :, whole], e2.at[slot, 0], right),
+            lambda: (give[slot].at[3, :, :, whole], e2.at[slot, 1], left),
+        )[kind]()
+        return pltpu.make_async_remote_copy(
+            src_ref=src,
+            dst_ref=dst,
+            send_sem=enc_send.at[slot, kind],
+            recv_sem=enc_recv.at[slot, kind],
+            device_id={"enc": to},
+            device_id_type=MESH,
+        )
+
+    def by_columns(action):
+        def one(a, carry):
+            for core in (0, 1):
+                action(a, core)
+            return carry
+
+        lax.fori_loop(0, RING, one, 0)
+
+    def enc_far(slot):
+        send, sum_of = give[slot], sums[slot]
+
+        def put_far(a, core, at, total):
+            send[0, a, core, low] = total[:half].astype(jnp.bfloat16)
+            send[1, a, core, low] = total[half:].astype(jnp.bfloat16)
+
+        def put_right(a, core, at, total):
+            sum_of[at] = total
+            send[2, a, core, high] = total[half:].astype(jnp.bfloat16)
+
+        def put_left(a, core, at, total):
+            sum_of[at] = total
+            send[3, a, core, low] = total[:half].astype(jnp.bfloat16)
+
+        def put_mine(a, core, at, total):
+            sum_of[at] = total
+
+        if slot == 0:
+            for pair in split:
+                pair_copies(pair, lambda copy: copy.wait())
+        product(slot, across(x), put_far)
+        enc_move(slot, 0).start()
+        enc_move(slot, 1).start()
+        product(slot, right, put_right)
+        product(slot, left, put_left)
+        product(slot, x, put_mine)
+
+    def enc_near(slot):
+        send, sum_of = give[slot], sums[slot]
+
+        def add_right(a, core):
+            total = sum_of[8 * right + 2 * a + core, low] + wide(e1[slot, 0, a, core])
+            send[2, a, core, low] = total.astype(jnp.bfloat16)
+
+        def add_left(a, core):
+            total = sum_of[8 * left + 2 * a + core, high] + wide(e1[slot, 1, a, core])
+            send[3, a, core, high] = total.astype(jnp.bfloat16)
+
+        enc_move(slot, 0).wait_recv()
+        by_columns(add_right)
+        enc_move(slot, 2).start()
+        enc_move(slot, 1).wait_recv()
+        by_columns(add_left)
+        enc_move(slot, 3).start()
+
+    def enc_done(slot):
+        enc_move(slot, 2).wait_recv()
+        enc_move(slot, 3).wait_recv()
+
+        for a in range(RING):
+            for core in (0, 1):
+                total = sums[slot][8 * x + 2 * a + core] + wide(e2[slot, 0, a, core]) + wide(e2[slot, 1, a, core])
+                n = 2 * a + core
+                enc_out[slot * NBR_LEN : (slot + 1) * NBR_LEN, n * HD : (n + 1) * HD] = total.astype(
+                    jnp.bfloat16
+                )
+        for kind in range(4):
+            enc_move(slot, kind).wait_send()
+
+    there = (
         (0, own_out),
         (1, block_on),
         (2, band_out),
         (3, band_on),
         (4, band_last),
-        (5, table_in),
-        (6, sibling_in),
-        (10, sum_block),
-        (9, sum_block_half),
-        (8, sum_band),
-        (7, sum_band_half),
-        (5, attend),
-        (6, sum_sibling),
+        (4, table_in),
     )
-
-    once = {0: rows_start, 3: rows_in, pairs + 4: tail_out, pairs + 5: rows_out}
+    back_small = ((9, sum_block), (8, sum_block_half))
+    back_large = ((7, sum_band), (6, sum_band_half))
+    turn = ((5, sibling_in), (4, attend), (5, sum_sibling))
+    leave = ((5, halves_out),)
+    between = {
+        12: (lambda: enc_far(0),),
+        13: (lambda: enc_near(0),),
+        14: (lambda: enc_far(1),),
+        15: (lambda: enc_near(1),),
+    }
+    after = {
+        0: (rows_start,),
+        3: (rows_in,),
+        7: (tail_out,),
+        8: (rows_out, lambda: pair_start(0, 1)),
+        9: (lambda: gather_pair(0), lambda: pair_start(2)),
+        10: (lambda: gather_pair(1), lambda: pair_start(3)),
+        15: (lambda: enc_done(0),),
+        16: (lambda: enc_done(1),),
+    }
+
+    def at_times(i, table):
+        for when, acts in table.items():
+
+            @pl.when(i == when)
+            def _(acts=acts):
+                for act in acts:
+                    act()
+
+    def run(i, stages, parts):
+        for lag, stage in stages:
+            for start, stop, skip, slots in parts:
+
+                @pl.when((i >= start + lag) & (i < stop + lag))
+                def _(lag=lag, stage=stage, skip=skip, slots=slots):
+                    for parity in (0, 1):
+                        stage(Head(2 * (i - lag - skip) + parity, parity, slots))
+
+    both = ((0, pairs, 0, (0, 1)),)
+    apart = (
+        (0, pairs - 2, 0, (0, 1)),
+        (pairs - 2, pairs, 0, (0,)),
+        (pairs, pairs + 2, 2, (1,)),
+    )
 
     def step(i, carry):
-        for lag, stage in stages:
-
-            @pl.when((i >= lag) & (i < pairs + lag))
-            def _(lag=lag, stage=stage):
-                for parity in (0, 1):
-                    stage(Head(2 * (i - lag) + parity, parity))
-
-        for when, act in once.items():
-            pl.when(i == when)(act)
+        run(i, there, both)
+        run(i, back_small, apart)
+        at_times(i, between)
+        run(i, back_large, apart)
+        run(i, turn, both)
+        run(i, leave, apart)
+        at_times(i, after)
         return carry
 
-    lax.fori_loop(0, pairs + max(lag for lag, _ in stages), step, 0)
+    lax.fori_loop(0, max(after) + 1, step, 0)
     for copy in result_copies():
         copy.wait()
 
@@ -554,15 +746,15 @@
         out_shape=[
             jax.ShapeDtypeStruct((rows, width), bf16),
             jax.ShapeDtypeStruct((rows, width), bf16),
-            jax.ShapeDtypeStruct((heads,) + tail, bf16),
+            jax.ShapeDtypeStruct((tail[1], depth // RING), bf16),
             jax.ShapeDtypeStruct((heads, RING, RING, 2) + rest, bf16),
             jax.ShapeDtypeStruct((heads,) + band, bf16),
         ],
         scratch_shapes=[
             pltpu.VMEM((RING, RING, 2) + rest, bf16),
             pltpu.VMEM((RING, RING, 2) + rest, bf16),
-            pltpu.VMEM((reads + 1, NBR_LEN, HD), f32),
-            pltpu.VMEM((reads + 1, NBR_LEN, HD), f32),
+            pltpu.VMEM((max(reads + 1, depth // HD), NBR_LEN, HD), f32),
+            pltpu.VMEM((max(reads + 1, depth // HD), NBR_LEN, HD), f32),
             pltpu.VMEM((heads,) + band, bf16),
             pltpu.VMEM(band, bf16),
             pltpu.VMEM(band, bf16),
@@ -577,10 +769,12 @@
             pltpu.VMEM((heads, 2, RING) + tail, bf16),
             pltpu.VMEM((heads, 2) + tail[1:], bf16),
             pltpu.VMEM((heads, 2) + tail, bf16),
+            pltpu.VMEM((2, 2, RING, 2, NBR_LEN // 2, HD), bf16),
+            pltpu.VMEM((2, 2, RING, 2, NBR_LEN, HD), bf16),
             dma((heads, 12)),
             dma((heads, 12)),
-            dma((heads, 9)),
-            dma((heads, 9)),
+            dma((heads, 17)),
+            dma((heads, 17)),
             dma((heads,)),
             dma((heads, 2)),
             dma((depth // HD,)),
@@ -588,133 +782,15 @@
             dma((4,)),
             dma((4,)),
             dma((4,)),
+            dma((heads // 2, 8)),
+            dma((2, 4)),
+            dma((2, 4)),
         ],
         compiler_params=pltpu.CompilerParams(
-            collective_id=0, has_side_effects=True, vmem_limit_bytes=63 * MIB
+            collective_id=0, has_side_effects=True, vmem_limit_bytes=64 * MIB
         ),
         name="core",
     )(ids, first, second, enc, w_key.reshape(folded), w_value.reshape(folded), queries, cotangents)
-
-
-def final_kernel(
-    grads, w_key, w_value, out, held, wide_right, wide_left, s1, s2, r1, r2, send_sem, recv_sem, w_sem
-):
-    x = lax.axis_index("enc")
-    right, left = up(x), down(x)
-    order = (across(x), right, left, x)
-    weights = (w_key, w_value)
-    heads = grads.shape[0]
-
-    def weight_copy(k, kv):
-        return pltpu.make_async_copy(weights[kv].at[order[k]], held.at[k, kv], w_sem.at[k, kv])
-
-    for k in range(RING):
-        for kv in (0, 1):
-            weight_copy(k, kv).start()
-    barrier = pltpu.get_barrier_semaphore()
-    for other in (right, left):
-        pl.semaphore_signal(barrier, inc=1, device_id={"enc": other}, device_id_type=MESH)
-    pl.semaphore_wait(barrier, 2)
-    rows, width = out.shape
-    half = rows // 2
-    strip = 256
-    lhs = [jnp.concatenate([grads[h, kv] for h in range(heads)], axis=1) for kv in (0, 1)]
-
-    def product(k, put):
-        for kv in (0, 1):
-            weight_copy(k, kv).wait()
-
-        def one(n, carry):
-            lines = pl.ds(pl.multiple_of(n * strip, strip), strip)
-            put(lines, sum(dot_t(lhs[kv], held[k, kv, lines, :]) for kv in (0, 1)))
-            return carry
-
-        lax.fori_loop(0, width // strip, one, 0)
-
-    def remote(kind, src, dst, to):
-        return pltpu.make_async_remote_copy(
-            src_ref=src,
-            dst_ref=dst,
-            send_sem=send_sem.at[kind],
-            recv_sem=recv_sem.at[kind],
-            device_id={"enc": to},
-            device_id_type=MESH,
-        )
-
-    moves = [
-        remote(0, s1.at[0], r1.at[0], right),
-        remote(1, s1.at[1], r1.at[1], left),
-        remote(2, s2.at[0], r2.at[0], right),
-        remote(3, s2.at[1], r2.at[1], left),
-    ]
-
-    def put_far(cols, part):
-        s1[0, :, cols] = part[:half].astype(jnp.bfloat16)
-        s1[1, :, cols] = part[half:].astype(jnp.bfloat16)
-
-    def put_right(cols, part):
-        wide_right[:, cols] = part[:half]
-        s2[0, pl.ds(half, half), cols] = part[half:].astype(jnp.bfloat16)
-
-    def put_left(cols, part):
-        s2[1, pl.ds(0, half), cols] = part[:half].astype(jnp.bfloat16)
-        wide_left[:, cols] = part[half:]
-
-    product(0, put_far)
-    moves[0].start()
-    moves[1].start()
-    product(1, put_right)
-    product(2, put_left)
-    moves[0].wait_recv()
-    s2[0, :half] = (wide_right[...] + wide(r1[0])).astype(jnp.bfloat16)
-    moves[2].start()
-    moves[1].wait_recv()
-    s2[1, half:] = (wide_left[...] + wide(r1[1])).astype(jnp.bfloat16)
-    moves[3].start()
-
-    def put_mine(cols, part):
-        wide_right[:, cols] = part[:half]
-        wide_left[:, cols] = part[half:]
-
-    product(3, put_mine)
-    moves[2].wait_recv()
-    moves[3].wait_recv()
-    for part, lines in ((wide_right, pl.ds(0, half)), (wide_left, pl.ds(half, half))):
-        total = part[...] + wide(r2[0, lines]) + wide(r2[1, lines])
-        out[lines] = total.astype(jnp.bfloat16)
-    for move in moves:
-        move.wait_send()
-
-
-def final(grads, w_key, w_value):
-    rows, width = grads.shape[2], w_key.shape[1]
-    half = rows // 2
-    bf16 = jnp.bfloat16
-    blocks = (RING, w_key.shape[0] // RING, width)
-    in_vmem = pl.BlockSpec(memory_space=pltpu.VMEM)
-    anywhere = pl.BlockSpec(memory_space=pl.ANY)
-    return pl.pallas_call(
-        final_kernel,
-        out_shape=jax.ShapeDtypeStruct((rows, blocks[1]), bf16),
-        in_specs=[in_vmem, anywhere, anywhere],
-        out_specs=in_vmem,
-        scratch_shapes=[
-            pltpu.VMEM((RING, 2) + blocks[1:], bf16),
-            pltpu.VMEM((half, blocks[1]), jnp.float32),
-            pltpu.VMEM((half, blocks[1]), jnp.float32),
-            pltpu.VMEM((2, half, blocks[1]), bf16),
-            pltpu.VMEM((2, rows, blocks[1]), bf16),
-            pltpu.VMEM((2, half, blocks[1]), bf16),
-            pltpu.VMEM((2, rows, blocks[1]), bf16),
-            pltpu.SemaphoreType.DMA((4,)),
-            pltpu.SemaphoreType.DMA((4,)),
-            pltpu.SemaphoreType.DMA((RING, 2)),
-        ],
-        compiler_params=pltpu.CompilerParams(
-            collective_id=1, has_side_effects=True, vmem_limit_bytes=48 * MIB
-        ),
-        name="final",
-    )(grads, w_key.reshape(blocks), w_value.reshape(blocks))
 
 
 def per_device(queries, d_attended, encodings, w_key, w_value, neighbour_owner, neighbour_slot):
@@ -732,11 +808,10 @@
     second = jnp.where(last > first, last, reads)
 
     enc_flat = encodings.reshape(owned * NBR_LEN, encodings.shape[2])
-    attended, d_queries, grads, _, _ = core(
+    attended, d_queries, d_encodings, _, _ = core(
         ids, first, second, enc_flat, w_key, w_value, queries, d_attended
     )
-    d_encodings = final(grads, w_key, w_value).reshape(owned, NBR_LEN, feat_width)
-    return (attended, d_queries, d_encodings)
+    return (attended, d_queries, d_encodings.reshape(owned, NBR_LEN, feat_width))
 
 
 def solution(mesh):

time: 231 us -> 221 us (0.957)
  Pallas kernels: 221 us -> 213 us
    pallas_call x1 -> x0, Pallas kernels: 22.8 us -> none  [final(): pl.pallas_call(final_kernel, out_shape=jax.ShapeDtypeStruct((rows, blocks...]
    pallas_call x1, Pallas kernels: 199 us -> 213 us  [core(): pl.pallas_call(core_kernel, in_specs=[in_smem] * 3 + [anywhere] * 5, out_...]
    unnamed x13 -> x11, local copies, waits for them, and re-layouts: 5.41 us -> 6.21 us
where the time goes in v5:
time: 221 us
  Pallas kernels  213 us (96%)
  local copies, waits for them, and re-layouts  6.39 us (3%)
    pallas_call x1, Pallas kernels, core(): pl.pallas_call(core_kernel, in_specs=[in_smem] * 3 + [anywhere] * 5, out_...  213 us
    unnamed x11, local copies, waits for them, and re-layouts  6.21 us

profile of v5, /device:TPU:1, one launch (start us, length us, event | category | flops | bytes accessed | tf_op | source)
XLA Modules:
  0.0 220.9 jit_solution(6189912681199552890)
XLA Ops:
  0.6 0.7 multiply_add_fusion
  1.3 0.1 copy.12
  1.4 0.1 reshape.22.ids
  1.5 0.0 copy-start.2
  1.5 0.5 copy-done.2
  2.0 0.1 select_reduce_fusion
  2.1 0.0 copy-start.3
  2.1 0.5 copy-done.3
  2.6 0.5 compare_select_fusion.second
  3.1 212.6 %core.1 = (bf16[896,1024]{1,0:T(8,128)(2,1)}, bf16[896,1024]{1,0:T(8,128)(2,1)}, bf16[256,1024]{1,0:T(8,128)(2,1)}, bf16[8,4,4,2,2,2,128,128]{7,6,5,4,3,2,1,0:T(8,128)(2,1)}, bf16[8,4,4,2,256,128]{5,4,3,2,1,0:T(8,128)(2,1)}) custom-call(s32[28]{0:T(128)} %copy-done.2, s32[64]{0:T(128)} %copy-done.3, s32[64]{0:T(128)} %compare_select_fusion.second, ...), custom_call_target="tpu_custom_call" | custom-call | tf_op jit(solution)/shard_map/core/pallas_call | solution.py:742
  215.7 0.0 copy-start
  215.7 3.0 %copy.16 = bf16[896,1024]{1,0:T(8,128)(2,1)} copy(bf16[896,1024]{1,0:T(8,128)(2,1)} %get-tuple-element.14) | data formatting | bytes 3670016
  218.7 0.0 copy-done
  218.7 0.0 copy-start.1
  218.8 1.2 copy.17
  220.0 0.2 copy-done.1
  220.1 0.8 copy.18
Async XLA Ops:
  1.5 0.5 copy-start.2
  2.1 0.5 copy-start.3
  215.7 3.0 %copy-start = (bf16[896,1024]{1,0:T(8,128)(2,1)S(1)}, bf16[896,1024]{1,0:T(8,128)(2,1)}, u32[]{:S(2)}) copy-start(bf16[896,1024]{1,0:T(8,128)(2,1)} %get-tuple-element.15) | copy-start | bytes 5505028
  218.7 1.4 copy-start.1

commit v6 on v5

--- a/solution.py
+++ b/solution.py
@@ -109,12 +109,12 @@
 
 
 def core_kernel(
-    ids, first, second, enc, w_key, w_value, queries, cotangents,
+    owner, slot_of, enc, w_key, w_value, queries, cotangents,
     att_out, dq_out, enc_out, tab, landed,
     table_even, table_odd, ck, cv, acc, give_even, give_odd, got_even, got_odd,
     own, q_buf, g_buf, att_buf, dq_buf, r1, r2, r3, r4, e1, e2,
     send_sem, recv_sem, back_send, back_recv, own_sem, load_sem,
-    enc_sem, w_sem, row_sem, rim_send, rim_recv, block_sem, enc_send, enc_recv,
+    enc_sem, w_sem, row_sem, rim_send, rim_recv, block_sem, enc_send, enc_recv, ids, first, second,
 ):
     x = lax.axis_index("enc")
     right, left = up(x), down(x)
@@ -202,6 +202,26 @@
             return carry
 
         lax.fori_loop(0, spans, one, 0)
+
+    def reads_in():
+        def one(s, carry):
+            for j in (0, 1):
+                ids[2 * s + j] = owner[j, s] * 2 + slot_of[j, s]
+            return carry
+
+        lax.fori_loop(0, spans, one, 0)
+
+        def find(n, carry):
+            hits = [ids[a] == n for a in range(reads)]
+            low_read, high_read = reads, -1
+            for a in range(reads):
+                high_read = jnp.where(hits[a], a, high_read)
+                low_read = jnp.where(hits[reads - 1 - a], reads - 1 - a, low_read)
+            first[n] = low_read
+            second[n] = jnp.where(high_read > low_read, high_read, reads)
+            return carry
+
+        lax.fori_loop(0, 2 * count, find, 0)
 
     def rows_start():
         for copy in row_copies():
@@ -572,14 +592,16 @@
         lax.fori_loop(0, RING, one, 0)
 
     half = NBR_LEN // 2
-    low, high, whole = pl.ds(0, half), pl.ds(half, half), pl.ds(0, NBR_LEN)
+    low, high = pl.ds(0, half), pl.ds(half, half)
 
     def enc_move(slot, kind):
         src, dst, to = (
             lambda: (give[slot].at[0, :, :, low], e1.at[slot, 0], right),
             lambda: (give[slot].at[1, :, :, low], e1.at[slot, 1], left),
-            lambda: (give[slot].at[2, :, :, whole], e2.at[slot, 0], right),
-            lambda: (give[slot].at[3, :, :, whole], e2.at[slot, 1], left),
+            lambda: (give[slot].at[2, :, :, low], e2.at[slot, 0, :, :, low], right),
+            lambda: (give[slot].at[3, :, :, high], e2.at[slot, 1, :, :, high], left),
+            lambda: (give[slot].at[2, :, :, high], e2.at[slot, 0, :, :, high], right),
+            lambda: (give[slot].at[3, :, :, low], e2.at[slot, 1, :, :, low], left),
         )[kind]()
         return pltpu.make_async_remote_copy(
             src_ref=src,
@@ -623,7 +645,9 @@
         enc_move(slot, 0).start()
         enc_move(slot, 1).start()
         product(slot, right, put_right)
+        enc_move(slot, 4).start()
         product(slot, left, put_left)
+        enc_move(slot, 5).start()
         product(slot, x, put_mine)
 
     def enc_near(slot):
@@ -645,8 +669,8 @@
         enc_move(slot, 3).start()
 
     def enc_done(slot):
-        enc_move(slot, 2).wait_recv()
-        enc_move(slot, 3).wait_recv()
+        for kind in (4, 5, 2, 3):
+            enc_move(slot, kind).wait_recv()
 
         for a in range(RING):
             for core in (0, 1):
@@ -655,7 +679,7 @@
                 enc_out[slot * NBR_LEN : (slot + 1) * NBR_LEN, n * HD : (n + 1) * HD] = total.astype(
                     jnp.bfloat16
                 )
-        for kind in range(4):
+        for kind in range(6):
             enc_move(slot, kind).wait_send()
 
     there = (
@@ -678,6 +702,7 @@
     }
     after = {
         0: (rows_start,),
+        2: (reads_in,),
         3: (rows_in,),
         7: (tail_out,),
         8: (rows_out, lambda: pair_start(0, 1)),
@@ -726,10 +751,10 @@
         copy.wait()
 
 
-def core(ids, first, second, enc, w_key, w_value, queries, cotangents):
+def core(owner, slot_of, enc, w_key, w_value, queries, cotangents):
     rows, width = queries.shape
     depth = enc.shape[1]
-    heads, reads = width // HD, ids.shape[0]
+    heads, reads = width // HD, 2 * owner.shape[1]
     rest = (2, 2, NBR_LEN, HD)
     tail = (2, 2 * NBR_LEN, HD)
     bf16, f32 = jnp.bfloat16, jnp.float32
@@ -741,7 +766,7 @@
     folded = (RING, RING, depth // (RING * RING), width)
     return pl.pallas_call(
         core_kernel,
-        in_specs=[in_smem] * 3 + [anywhere] * 5,
+        in_specs=[in_smem] * 2 + [anywhere] * 5,
         out_specs=[anywhere, anywhere, in_vmem, anywhere, anywhere],
         out_shape=[
             jax.ShapeDtypeStruct((rows, width), bf16),
@@ -783,33 +808,25 @@
             dma((4,)),
             dma((4,)),
             dma((heads // 2, 8)),
-            dma((2, 4)),
-            dma((2, 4)),
+            dma((2, 6)),
+            dma((2, 6)),
+            pltpu.SMEM((reads,), jnp.int32),
+            pltpu.SMEM((4 * RING * RING,), jnp.int32),
+            pltpu.SMEM((4 * RING * RING,), jnp.int32),
         ],
         compiler_params=pltpu.CompilerParams(
             collective_id=0, has_side_effects=True, vmem_limit_bytes=64 * MIB
         ),
         name="core",
-    )(ids, first, second, enc, w_key.reshape(folded), w_value.reshape(folded), queries, cotangents)
+    )(owner, slot_of, enc, w_key.reshape(folded), w_value.reshape(folded), queries, cotangents)
 
 
 def per_device(queries, d_attended, encodings, w_key, w_value, neighbour_owner, neighbour_slot):
-    tok_rows, feat_width = queries.shape
-    heads = feat_width // HD
+    feat_width = queries.shape[1]
     owned = encodings.shape[0]
-    owners = lax.axis_size("seq")
-    reads = 2 * (tok_rows // SPAN)
-
-    ids = (neighbour_owner * owned + neighbour_slot).reshape(reads).astype(jnp.int32)
-    hit = ids[None, :] == jnp.arange(owners * owned, dtype=jnp.int32)[:, None]
-    order = jnp.arange(reads, dtype=jnp.int32)[None, :]
-    first = jnp.min(jnp.where(hit, order, reads), axis=1)
-    last = jnp.max(jnp.where(hit, order, -1), axis=1)
-    second = jnp.where(last > first, last, reads)
-
     enc_flat = encodings.reshape(owned * NBR_LEN, encodings.shape[2])
     attended, d_queries, d_encodings, _, _ = core(
-        ids, first, second, enc_flat, w_key, w_value, queries, d_attended
+        neighbour_owner.T, neighbour_slot.T, enc_flat, w_key, w_value, queries, d_attended
     )
     return (attended, d_queries, d_encodings.reshape(owned, NBR_LEN, feat_width))
 

time: 221 us -> 216 us (0.977)
  Pallas kernels: 213 us -> 210 us
    pallas_call x1, Pallas kernels: 213 us -> 210 us  [core(): pl.pallas_call(core_kernel, in_specs=[in_smem] * 2 + [anywhere] * 5, out_...]
    unnamed x11 -> x7, local copies, waits for them, and re-layouts: 6.21 us -> 5.2 us
where the time goes in v6:
time: 216 us
  Pallas kernels  210 us (97%)
  local copies, waits for them, and re-layouts  5.2 us (2%)
    pallas_call x1, Pallas kernels, core(): pl.pallas_call(core_kernel, in_specs=[in_smem] * 2 + [anywhere] * 5, out_...  210 us
    unnamed x7, local copies, waits for them, and re-layouts  5.2 us

profile of v6, /device:TPU:1, one launch (start us, length us, event | category | flops | bytes accessed | tf_op | source)
XLA Modules:
  0.0 215.9 jit_solution(5142762362890694748)
XLA Ops:
  0.6 210.0 %core.1 = (bf16[896,1024]{1,0:T(8,128)(2,1)}, bf16[896,1024]{1,0:T(8,128)(2,1)}, bf16[256,1024]{1,0:T(8,128)(2,1)}, bf16[8,4,4,2,2,2,128,128]{7,6,5,4,3,2,1,0:T(8,128)(2,1)}, bf16[8,4,4,2,256,128]{5,4,3,2,1,0:T(8,128)(2,1)}) custom-call(s32[2,14]{1,0:T(2,128)} %bitcast.10, s32[2,14]{1,0:T(2,128)} %bitcast.11, bf16[256,4096]{1,0:T(8,128)(2,1)} %bitcast.8, ...), custom_call_target="tpu_custom_call" | custom-call | tf_op jit(solution)/shard_map/core/pallas_call | solution.py:767
  210.6 0.0 copy-start
  210.7 3.0 %copy.13 = bf16[896,1024]{1,0:T(8,128)(2,1)} copy(bf16[896,1024]{1,0:T(8,128)(2,1)} %get-tuple-element.12) | data formatting | bytes 3670016
  213.7 0.0 copy-done
  213.7 0.0 copy-start.1
  213.7 1.2 copy.14
  214.9 0.2 copy-done.1
  215.1 0.8 copy.15
Async XLA Ops:
  210.6 3.0 %copy-start = (bf16[896,1024]{1,0:T(8,128)(2,1)S(1)}, bf16[896,1024]{1,0:T(8,128)(2,1)}, u32[]{:S(2)}) copy-start(bf16[896,1024]{1,0:T(8,128)(2,1)} %get-tuple-element.13) | copy-start | bytes 5505028
  213.7 1.4 copy-start.1

commit v7 on v6

--- a/solution.py
+++ b/solution.py
@@ -821,6 +821,26 @@
     )(owner, slot_of, enc, w_key.reshape(folded), w_value.reshape(folded), queries, cotangents)
 
 
+def hand_out_kernel(*refs):
+    count = len(refs) // 2
+    for source, target in zip(refs[:count], refs[count:]):
+        target[...] = source[...]
+
+
+def hand_out(*values):
+    parts = 4
+    specs = [pl.BlockSpec((v.shape[0] // parts, v.shape[1]), lambda i: (i, 0)) for v in values]
+    return pl.pallas_call(
+        hand_out_kernel,
+        grid=(parts,),
+        in_specs=specs,
+        out_specs=specs,
+        out_shape=[jax.ShapeDtypeStruct(v.shape, v.dtype) for v in values],
+        compiler_params=pltpu.CompilerParams(vmem_limit_bytes=62 * MIB),
+        name="hand_out",
+    )(*values)
+
+
 def per_device(queries, d_attended, encodings, w_key, w_value, neighbour_owner, neighbour_slot):
     feat_width = queries.shape[1]
     owned = encodings.shape[0]
@@ -828,6 +848,7 @@
     attended, d_queries, d_encodings, _, _ = core(
         neighbour_owner.T, neighbour_slot.T, enc_flat, w_key, w_value, queries, d_attended
     )
+    attended, d_queries, d_encodings = hand_out(attended, d_queries, d_encodings)
     return (attended, d_queries, d_encodings.reshape(owned, NBR_LEN, feat_width))
 
 

time: 216 us -> 216 us (level)
  local copies, waits for them, and re-layouts: 5.2 us -> 0 us
  Pallas kernels: 210 us -> 215 us
    unnamed x7 -> x0, local copies, waits for them, and re-layouts: 5.2 us -> none
    pallas_call x0 -> x1, Pallas kernels: none -> 4.65 us  [hand_out(): pl.pallas_call(hand_out_kernel, grid=(parts,), in_specs=specs, out_specs=...]
where the time goes in v7:
time: 216 us; the launch traced here: 215 us
  Pallas kernels  215 us (100%)
    pallas_call x1, Pallas kernels, core(): pl.pallas_call(core_kernel, in_specs=[in_smem] * 2 + [anywhere] * 5, out_...  210 us
    pallas_call x1, Pallas kernels, hand_out(): pl.pallas_call(hand_out_kernel, grid=(parts,), in_specs=specs, out_specs=...  4.65 us

profile of v7, /device:TPU:1, one launch (start us, length us, event | category | flops | bytes accessed | tf_op | source)
XLA Modules:
  0.0 215.3 jit_solution(17407915281116898026)
XLA Ops:
  0.6 210.0 %core.1 = (bf16[896,1024]{1,0:T(8,128)(2,1)}, bf16[896,1024]{1,0:T(8,128)(2,1)}, bf16[256,1024]{1,0:T(8,128)(2,1)}, bf16[8,4,4,2,2,2,128,128]{7,6,5,4,3,2,1,0:T(8,128)(2,1)}, bf16[8,4,4,2,256,128]{5,4,3,2,1,0:T(8,128)(2,1)}) custom-call(s32[2,14]{1,0:T(2,128)} %bitcast.9, s32[2,14]{1,0:T(2,128)} %bitcast.10, bf16[256,4096]{1,0:T(8,128)(2,1)} %bitcast.8, ...), custom_call_target="tpu_custom_call" | custom-call | tf_op jit(solution)/shard_map/core/pallas_call | solution.py:767
  210.6 4.6 %hand_out.1 = (bf16[896,1024]{1,0:T(8,128)(2,1)}, bf16[896,1024]{1,0:T(8,128)(2,1)}, bf16[256,1024]{1,0:T(8,128)(2,1)}) custom-call(bf16[896,1024]{1,0:T(8,128)(2,1)} %get-tuple-element.9.refs_0_, bf16[896,1024]{1,0:T(8,128)(2,1)} %get-tuple-element.10.refs_1_, bf16[256,1024]{1,0:T(8,128)(2,1)} %get-tuple-element.11.refs_2_), custom_call_target="tpu_custom_call" | custom-call | tf_op jit(solution)/shard_map/hand_out/pallas_call | solution.py:833
